TPU v7x, 128 devices: a whole 4x4x4 slice. The times are simulated.
128 devices in a mesh: lat: 4 (over z), lon: 32 (over x, y, core).
Axes of the slice: x: 4, y: 4, z: 4, core: 2. Of those that a mesh axis runs over, the one named last changes fastest.
Arguments:
- observations: float32 [1572864, 32], P(('lat', 'lon')), may hold values from -6 to 6
- destinations: int32 [1572864, 1], P(('lat', 'lon')), may hold values from 0 to 127; in each aligned block of 12288 rows (0 to 12287, 12288 to 24575, ...) at most 192 rows name the same one
- cells: int32 [1572864], P(('lat', 'lon')), may hold values from 0 to 1151
- first_weight: float32 [32, 256], replicated, may hold values from -1 to 1
- first_bias: float32 [256], replicated, may hold values from -3 to 3
- second_weight: bfloat16 [256, 256], replicated, may hold values from -0.375 to 0.375
- conv_first: bfloat16 [3, 3, 256, 256], replicated, may hold values from -0.125 to 0.125
- conv_bias: float32 [256], replicated, may hold values from -3 to 3
- conv_second: bfloat16 [3, 3, 256, 256], replicated, may hold values from -0.125 to 0.125
Outputs:
- encoded: bfloat16 [96, 1536, 256], P('lat', 'lon')
Inputs may be any that keep to these rules, and one draw needn't show every extreme that they name: `destinations`: within the rows of one ingest shard, no tile is named by more than 192 rows, a bound that some block reaches.
All inputs are finite; a program needn't handle non-finite values.
Results may differ from a plain program's by a relative error of at most 0.015.
Values may be sent and summed in bfloat16 or wider, within the bound.
A program may use at most 128 MiB of HBM per device.

v0:
```python
import functools
import math

import jax
import jax.numpy as jnp
from jax import lax
from jax.experimental import pallas as pl
from jax.experimental.pallas import tpu as pltpu
from jax.sharding import PartitionSpec as P

TILE_ROWS = 24
TILE_COLS = 48
BLOCK = 256


def with_halo(cells, sides, width, closed):
    for axis, dim in sides:
        count = lax.axis_size(axis)
        ends = count if closed else count - 1
        head = lax.slice_in_dim(cells, 0, width, axis=dim)
        tail = lax.slice_in_dim(cells, cells.shape[dim] - width, cells.shape[dim], axis=dim)
        cells = jnp.concatenate(
            [
                lax.ppermute(tail, axis, [(i, (i + 1) % count) for i in range(ends)]),
                cells,
                lax.ppermute(head, axis, [((i + 1) % count, i) for i in range(ends)]),
            ],
            axis=dim,
        )
    return cells


def shifted(shard, axis, by):
    count = lax.axis_size(axis)
    return lax.ppermute(shard, axis, [(i, (i + by) % count) for i in range(count)])


def convolve(tile, kernel):
    padded = with_halo(tile, (("lat", 0),), 1, False)
    edges = jnp.stack([tile[0], tile[-1]])
    partner = shifted(edges, "lon", lax.axis_size("lon") // 2)
    band = lax.axis_index("lat")
    upper = jnp.where(band == 0, partner[0], padded[0])
    lower = jnp.where(band == lax.axis_size("lat") - 1, partner[1], padded[-1])
    padded = jnp.concatenate([upper[None], tile, lower[None]], axis=0)
    padded = with_halo(padded, (("lon", 1),), 1, True)
    tile_rows = tile.shape[0]
    tile_cols = tile.shape[1]
    width = tile.shape[2]
    total = jnp.zeros((tile_rows * tile_cols, kernel.shape[3]), jnp.float32)
    for row_tap in range(3):
        for col_tap in range(3):
            window = padded[row_tap : row_tap + tile_rows, col_tap : col_tap + tile_cols].reshape(
                -1, width
            )
            total = total + jnp.dot(
                window, kernel[row_tap, col_tap], preferred_element_type=jnp.float32
            )
    return total.reshape(tile_rows, tile_cols, -1)


def dispatch_kernel(shards, capacity, unroll, obs_ref, dest_ref, cell_ref, rows_ref, cells_ref,
                    source, slots, table, places, places_smem, copy_sem):
    values, count_rows = obs_ref.shape
    packing = 128 // values
    packed = capacity // packing
    planes = shards * packed
    blocks = count_rows // BLOCK
    f32, bf16, i32 = jnp.float32, jnp.bfloat16, jnp.int32

    lane = lax.broadcasted_iota(i32, (BLOCK, BLOCK + 128), 1)
    row = lax.broadcasted_iota(i32, (BLOCK, BLOCK + 128), 0)
    earlier = jnp.where((row < lane) | (lane >= BLOCK), 1.0, 0.0).astype(bf16)
    value_lane = lax.broadcasted_iota(i32, (values, 128), 1)
    value_row = lax.broadcasted_iota(i32, (values, 128), 0)
    spread = jnp.where(lax.rem(value_lane, values) == value_row, 1.0, 0.0).astype(bf16)
    tile_row = lax.broadcasted_iota(i32, (shards, BLOCK), 0)
    rank_row = lax.broadcasted_iota(i32, (capacity, BLOCK), 0).astype(f32)

    table[...] = jnp.zeros_like(table)

    def rank_block(block, carry):
        at = pl.multiple_of(block * BLOCK, BLOCK)
        dest = dest_ref[:, pl.ds(at, BLOCK)]
        cell = cell_ref[:, pl.ds(at, BLOCK)]
        named = jnp.where(tile_row == dest, 1.0, 0.0)
        counted = jnp.dot(named.astype(bf16), earlier, preferred_element_type=f32)
        before = counted[:, :BLOCK] + jnp.concatenate([carry] * (BLOCK // 128), axis=1)
        rank = jnp.sum(named * before, axis=0, keepdims=True)
        rank_whole = rank.astype(i32)
        plane = jnp.where(rank_whole >= packed, 1, 0)
        for cut in range(2, packing):
            plane = plane + jnp.where(rank_whole >= cut * packed, 1, 0)
        places[:, pl.ds(at, BLOCK)] = dest * packed + rank_whole + plane * (planes - packed)
        high = lax.shift_right_logical(cell, 6)
        low = cell - lax.shift_left(high, 6)
        weights = jnp.concatenate(
            [named * (high + 1).astype(f32), named * low.astype(f32)], axis=0
        ).astype(bf16)
        ranked = jnp.where(rank_row == rank, 1.0, 0.0).astype(bf16)
        table[...] += lax.dot_general(
            weights, ranked, (((1,), (1,)), ((), ())), preferred_element_type=f32
        )
        source[pl.ds(at, BLOCK), :] = lax.dot_general(
            obs_ref[:, pl.ds(at, BLOCK)].astype(bf16),
            spread,
            (((0,), (0,)), ((), ())),
            preferred_element_type=f32,
        )
        zero_at = pl.multiple_of(block * (packing * planes // blocks), 8)
        slots[pl.ds(zero_at, packing * planes // blocks), :] = jnp.zeros(
            (packing * planes // blocks, 128), f32
        )
        return carry + counted[:, BLOCK:]

    lax.fori_loop(0, blocks, rank_block, jnp.zeros((shards, 128), f32), unroll=4)

    copy = pltpu.make_async_copy(places, places_smem, copy_sem)
    copy.start()
    found = table[:shards, :].astype(i32) * 64 + table[shards:, :].astype(i32) - 64
    found = jnp.where(found >= 0, found, -1)
    absent = jnp.full((shards, 64), -1, i32)
    straight = jnp.concatenate([found, absent], axis=1)
    turned = jnp.concatenate([absent, found], axis=1)
    turn = lax.rem(lax.broadcasted_iota(i32, (shards, 1), 0) + lax.axis_index("lon"), 2)
    placed = jnp.where(turn == 1, turned, straight)
    cells_ref[:, 0, :] = placed[:, :128]
    cells_ref[:, 1, :] = placed[:, 128:]
    copy.wait()

    def move(step, _):
        at = pl.multiple_of(step * unroll, unroll)
        for k in range(unroll):
            place = places_smem[0, at + k]
            slots[pl.ds(place, 1), :] = source[pl.ds(at + k, 1), :]
        return 0

    lax.fori_loop(0, count_rows // unroll, move, 0)

    group = lax.broadcasted_iota(i32, (packed, 128), 1) // values

    def pack(dest, _):
        at = pl.multiple_of(dest * packed, packed)
        total = slots[pl.ds(at, packed), :]
        for plane in range(1, packing):
            total = jnp.where(group == plane, slots[pl.ds(plane * planes + at, packed), :], total)
        rows_ref[dest] = total.astype(bf16)
        return 0

    lax.fori_loop(0, shards, pack, 0, unroll=2)


def dispatch(obs, dest, cells, shards, capacity, unroll=64):
    count_rows, values = obs.shape
    packing = 128 // values
    packed = capacity // packing
    vmem = pl.BlockSpec(memory_space=pltpu.VMEM)
    return pl.pallas_call(
        functools.partial(dispatch_kernel, shards, capacity, unroll),
        out_shape=(
            jax.ShapeDtypeStruct((shards, packed, 128), jnp.bfloat16),
            jax.ShapeDtypeStruct((shards, 2, 128), jnp.int32),
        ),
        in_specs=[vmem] * 3,
        out_specs=[vmem] * 2,
        scratch_shapes=[
            pltpu.VMEM((count_rows, 128), jnp.float32),
            pltpu.VMEM((shards * capacity, 128), jnp.float32),
            pltpu.VMEM((2 * shards, capacity), jnp.float32),
            pltpu.VMEM((1, count_rows), jnp.int32),
            pltpu.SMEM((1, count_rows), jnp.int32),
            pltpu.SemaphoreType.DMA,
        ],
        compiler_params=pltpu.CompilerParams(vmem_limit_bytes=48 * 1024 * 1024),
        name="dispatch",
    )(obs.T, dest.reshape(1, -1), cells.reshape(1, -1))


def place_of(step, bands, sector_dims):
    digits = []
    for size in reversed(sector_dims):
        digits.append(lax.rem(step, size))
        step = lax.div(step, size)
    return step, digits[::-1]


def partner(step, sign, bands, sector_dims):
    band_step, steps = place_of(step, bands, sector_dims)
    _, mine = place_of(lax.axis_index("lon"), 1, sector_dims)
    band = lax.rem(lax.axis_index("lat") + (band_step if sign > 0 else bands - band_step), bands)
    sector = 0
    for size, digit, own in zip(sector_dims, steps, mine):
        sector = sector * size + lax.rem(own + (digit if sign > 0 else size - digit), size)
    return band, sector


def exchange_kernel(bands, sector_dims, group, chunk, rows_ref, cells_ref, first_ref, bias_ref, second_ref, latent_ref,
                    rows_got, cells_got, features, sums, counts, own_sem, send_rows, send_cells, recv_rows, recv_cells):
    shards, packed, _ = rows_got.shape
    values = first_ref.shape[0]
    width = second_ref.shape[1]
    packing = 128 // values
    capacity = packing * packed
    sectors = math.prod(sector_dims)
    tile_cells = TILE_ROWS * TILE_COLS
    f32, bf16, i32 = jnp.float32, jnp.bfloat16, jnp.int32
    mesh_id = pl.DeviceIdType.MESH

    barrier = pltpu.get_barrier_semaphore()

    def greet(step, _):
        pl.semaphore_signal(barrier, inc=1, device_id=partner(step, 1, bands, sector_dims), device_id_type=mesh_id)
        return 0

    lax.fori_loop(1, shards, greet, 0)
    pl.semaphore_wait(barrier, shards - 1)

    def copies(step):
        band, sector = partner(step, 1, bands, sector_dims)
        target = band * sectors + sector
        return (
            pltpu.make_async_remote_copy(
                src_ref=rows_ref.at[target], dst_ref=rows_got.at[step], send_sem=send_rows.at[step],
                recv_sem=recv_rows.at[step], device_id=(band, sector), device_id_type=mesh_id),
            pltpu.make_async_remote_copy(
                src_ref=cells_ref.at[target], dst_ref=cells_got.at[step], send_sem=send_cells.at[step],
                recv_sem=recv_cells.at[step], device_id=(band, sector), device_id_type=mesh_id),
        )

    def send(step, _):
        for copy in copies(step):
            copy.start()
        return 0

    me = lax.axis_index("lat") * sectors + lax.axis_index("lon")
    own_rows = pltpu.make_async_copy(rows_ref.at[me], rows_got.at[0], own_sem.at[0])
    own_cells = pltpu.make_async_copy(cells_ref.at[me], cells_got.at[0], own_sem.at[1])
    own_rows.start()
    own_cells.start()
    lax.fori_loop(1, shards, send, 0)

    sums[...] = jnp.zeros_like(sums)
    counts[...] = jnp.zeros_like(counts)
    first = first_ref[...]
    first_high = first.astype(bf16)
    first_low = (first - first_high.astype(f32)).astype(bf16)
    blank = jnp.zeros((values, width), bf16)
    weights = []
    for plane in range(packing):
        pieces = [blank] * (2 * packing)
        pieces[plane] = first_high
        pieces[packing + plane] = first_low
        weights.append(jnp.concatenate(pieces, axis=0))
    half_bias = 0.5 * bias_ref[...]
    own_rows.wait()
    own_cells.wait()

    lane = lax.broadcasted_iota(i32, (1, 128), 1)

    def receive(step, _):
        for copy in copies(step):
            copy.wait_recv()
        return 0

    def work(number, _):
        base = number * group
        lax.fori_loop(jnp.maximum(base, 1), base + group, receive, 0)
        rows = rows_got[pl.ds(base, group)].reshape(group * packed, 128)
        rows = jnp.concatenate([rows, rows], axis=1)
        for plane in range(packing):
            half = 0.5 * jnp.dot(rows, weights[plane], preferred_element_type=f32) + half_bias
            hidden = (half + half * jnp.tanh(half)).astype(bf16)
            made = jnp.dot(hidden, second_ref[...], preferred_element_type=f32).astype(bf16)
            features[:, plane] = made.reshape(group, packed, width)
        for part in range(group // chunk):
            pieces = []
            for pair in range(part * chunk // 2, (part + 1) * chunk // 2):
                even = cells_got[base + 2 * pair]
                odd = cells_got[base + 2 * pair + 1]
                pieces += [even[0:1], jnp.where(lane < 64, even[1:2], odd[0:1]), odd[1:2]]
            cell = jnp.concatenate(pieces, axis=1)
            span = chunk * capacity
            spots = lax.broadcasted_iota(jnp.int16, (tile_cells, span), 0)
            onehot = jnp.where(spots == cell.astype(jnp.int16), 1.0, 0.0).astype(bf16)
            sums[...] += jnp.dot(
                onehot, features[pl.ds(part * chunk, chunk)].reshape(span, width), preferred_element_type=f32)
            line = lax.shift_right_arithmetic(cell * 1366, 16)
            column = cell - line * TILE_COLS
            lines = jnp.where(lax.broadcasted_iota(i32, (32, span), 0) == line, 1.0, 0.0).astype(bf16)
            columns = jnp.where(
                (lax.broadcasted_iota(i32, (TILE_COLS, span), 0) == column) & (cell >= 0), 1.0, 0.0).astype(bf16)
            counts[...] += lax.dot_general(columns, lines, (((1,), (1,)), ((), ())), preferred_element_type=f32)
        return 0

    lax.fori_loop(0, shards // group, work, 0)

    scale = 1.0 / jnp.maximum(counts[...], 1.0)
    for line in range(TILE_ROWS):
        block = sums[pl.ds(line * TILE_COLS, TILE_COLS), :] * scale[:, line:line + 1]
        latent_ref[line] = block.astype(bf16)

    def drain(step, _):
        for copy in copies(step):
            copy.wait_send()
        return 0

    lax.fori_loop(1, shards, drain, 0)


def exchange(rows, cells, first_weight, first_bias, second_weight, bands, sector_dims, group=16, chunk=4):
    shards, packed, _ = rows.shape
    width = second_weight.shape[1]
    vmem = pl.BlockSpec(memory_space=pltpu.VMEM)
    anywhere = pl.BlockSpec(memory_space=pl.ANY)
    packing = 128 // first_weight.shape[0]
    dma = pltpu.SemaphoreType.DMA
    return pl.pallas_call(
        functools.partial(exchange_kernel, bands, sector_dims, group, chunk),
        out_shape=jax.ShapeDtypeStruct((TILE_ROWS, TILE_COLS, width), jnp.bfloat16),
        in_specs=[anywhere, anywhere, vmem, vmem, vmem],
        out_specs=vmem,
        scratch_shapes=[
            pltpu.VMEM((shards, packed, 128), jnp.bfloat16),
            pltpu.VMEM((shards, 2, 128), jnp.int32),
            pltpu.VMEM((group, packing, packed, width), jnp.bfloat16),
            pltpu.VMEM((TILE_ROWS * TILE_COLS, width), jnp.float32),
            pltpu.VMEM((TILE_COLS, 32), jnp.float32),
            dma((2,)), dma((shards,)), dma((shards,)), dma((shards,)), dma((shards,)),
        ],
        compiler_params=pltpu.CompilerParams(
            collective_id=0, has_side_effects=True, vmem_limit_bytes=48 * 1024 * 1024),
        name="exchange",
    )(rows, cells, first_weight, first_bias.reshape(1, -1), second_weight)


def body(
    observations,
    destinations,
    cells,
    first_weight,
    first_bias,
    second_weight,
    conv_first,
    conv_bias,
    conv_second,
):
    bands = lax.axis_size("lat")
    sectors = lax.axis_size("lon")
    shards = bands * sectors
    capacity = 2 * observations.shape[0] // shards
    rows, spots = dispatch(observations, destinations, cells, shards, capacity)
    latent = exchange(rows, spots, first_weight, first_bias, second_weight, bands, (4, 4, 2))
    middle = jax.nn.silu(convolve(latent, conv_first) + conv_bias).astype(jnp.bfloat16)
    return (latent.astype(jnp.float32) + convolve(middle, conv_second)).astype(jnp.bfloat16)


def solution(mesh):
    in_specs = (
        P(("lat", "lon"), None),
        P(("lat", "lon"), None),
        P(("lat", "lon")),
        P(),
        P(),
        P(),
        P(),
        P(),
        P(),
    )
    out_specs = P("lat", "lon", None)
    return jax.shard_map(body, mesh=mesh, in_specs=in_specs, out_specs=out_specs, check_vma=False)
```

profile of v0, /device:TPU:0, one launch (start us, length us, event | category | flops | bytes accessed | tf_op | source)
XLA Modules:
  0.0 124.5 jit_solution(4216147749853154190)
XLA Ops:
  0.0 0.0 copy-start.5
  0.0 0.0 copy-start
  0.0 1.4 %copy-done = f32[12288,32]{0,1:T(8,128)S(1)} copy-done((f32[12288,32]{0,1:T(8,128)S(1)}, f32[12288,32]{0,1:T(8,128)}, u32[]{:S(2)}) %copy-start) | copy-done | bytes 1572888
  1.4 0.8 copy-done.2
  2.2 0.0 copy-start.3
  2.2 0.8 copy-done.3
  3.0 23.6 %dispatch.1 = (bf16[128,48,128]{2,1,0:T(8,128)(2,1)S(1)}, s32[128,2,128]{2,1,0:T(2,128)S(1)}) custom-call(f32[32,12288]{1,0:T(8,128)S(1)} %bitcast.95, s32[1,12288]{1,0:T(1,128)S(1)} %bitcast.96, s32[1,12288]{1,0:T(1,128)S(1)} %bitcast.97), custom_call_target="tpu_custom_call" | custom-call | tf_op jit(solution)/shard_map/dispatch/pallas_call | solution.py:158
  26.6 0.0 copy-done.5
  26.6 0.0 copy-done.1
  26.6 0.0 copy-done.4
  26.6 54.7 %exchange.1 = bf16[24,48,256]{2,1,0:T(8,128)(2,1)S(1)} custom-call(bf16[128,48,128]{2,1,0:T(8,128)(2,1)S(1)} %get-tuple-element.7.rows_ref, s32[128,2,128]{2,1,0:T(2,128)S(1)} %get-tuple-element.8.cells_ref, f32[32,256]{1,0:T(8,128)S(1)} %copy-done.4, f32[1,256]{1,0:T(1,128)S(1)} %bitcast.98, bf16[256,256]{1,0:T(8,128)(2,1)S(1)} %copy-done.1), custom_call_target="tpu_custom_call" | custom-call | tf_op jit(solution)/shard_map/exchange/pallas_call | solution.py:317
  81.4 0.6 collective-permute-start
  82.0 3.0 %collective-permute-start.1 = (bf16[1,48,256]{2,1,0:T(8,128)(2,1)S(1)}, bf16[1,48,256]{2,1,0:T(8,128)(2,1)S(1)}, u32[]{:S(2)}, u32[]{:S(2)}) collective-permute-start(bf16[1,48,256]{2,1,0:T(8,128)(2,1)S(1)} %get-tuple-element.36), channel_id=1, source_target_pairs={{0,32},{32,64},{64,96},{1,33},{33,65},{65,97},{2,34},{34,66},{66,9... | collective-permute-start | bytes 73736 | tf_op jit(solution)/shard_map/ppermute | solution.py:24
  85.0 1.3 %collective-permute-start.2 = (bf16[1,48,256]{2,1,0:T(8,128)(2,1)S(1)}, bf16[1,48,256]{2,1,0:T(8,128)(2,1)S(1)}, u32[]{:S(2)}, u32[]{:S(2)}) collective-permute-start(bf16[1,48,256]{2,1,0:T(8,128)(2,1)S(1)} %get-tuple-element.35), channel_id=1, source_target_pairs={{32,0},{64,32},{96,64},{33,1},{65,33},{97,65},{34,2},{66,34},{98,6... | collective-permute-start | bytes 73736 | tf_op jit(solution)/shard_map/ppermute | solution.py:26
  86.3 0.2 collective-permute-done.1
  86.5 4.2 %collective-permute-done.2 = bf16[1,48,256]{2,1,0:T(8,128)(2,1)S(1)} collective-permute-done((bf16[1,48,256]{2,1,0:T(8,128)(2,1)S(1)}, bf16[1,48,256]{2,1,0:T(8,128)(2,1)S(1)}, u32[]{:S(2)}, u32[]{:S(2)}) %collective-permute-start.2) | collective-permute-done | bytes 24608 | tf_op jit(solution)/shard_map/ppermute | solution.py:26
  90.7 0.0 collective-permute-done
  90.7 0.0 copy-start.6
  90.8 0.1 pad_maximum_fusion.4
  90.9 4.1 %collective-permute-start.3 = (bf16[26,1,256]{2,1,0:T(2,128)(2,1)S(1)}, bf16[26,1,256]{2,1,0:T(2,128)(2,1)S(1)}, u32[]{:S(2)}, u32[]{:S(2)}) collective-permute-start(bf16[26,1,256]{2,1,0:T(2,128)(2,1)S(1)} %get-tuple-element.28), channel_id=1, source_target_pairs={{0,1},{1,2},{2,3},{3,4},{4,5},{5,6},{6,7},{7,8},{8,9},{9,10},{10,1... | collective-permute-start | bytes 39944 | tf_op jit(solution)/shard_map/ppermute | solution.py:24
  95.0 2.9 %collective-permute-start.4 = (bf16[26,1,256]{2,1,0:T(2,128)(2,1)S(1)}, bf16[26,1,256]{2,1,0:T(2,128)(2,1)S(1)}, u32[]{:S(2)}, u32[]{:S(2)}) collective-permute-start(bf16[26,1,256]{2,1,0:T(2,128)(2,1)S(1)} %get-tuple-element.27), channel_id=1, source_target_pairs={{1,0},{2,1},{3,2},{4,3},{5,4},{6,5},{7,6},{8,7},{9,8},{10,9},{11,1... | collective-permute-start | bytes 39944 | tf_op jit(solution)/shard_map/ppermute | solution.py:26
  97.9 0.0 copy-done.6
  97.9 0.3 fusion.19
  98.2 1.1 collective-permute-done.3
  99.3 0.1 collective-permute-done.4
  99.4 0.5 pad_maximum_fusion
  99.9 0.4 fusion.43
  100.3 0.3 convolution_add_fusion.15
  100.6 0.3 convolution_add_fusion.14
  100.9 0.3 convolution_add_fusion.13
  101.3 0.3 convolution_add_fusion.12
  101.6 0.3 convolution_add_fusion.11
  101.9 0.3 convolution_add_fusion.10
  102.2 0.3 convolution_add_fusion.9
  102.5 0.0 copy-start.8
  102.6 0.3 convolution_add_fusion.8
  102.9 0.4 copy-done.8
  103.2 0.3 multiply_convert_fusion.1
  103.6 0.1 collective-permute-start.5
  103.7 3.6 %collective-permute-start.6 = (bf16[1,48,256]{2,1,0:T(8,128)(2,1)S(1)}, bf16[1,48,256]{2,1,0:T(8,128)(2,1)S(1)}, u32[]{:S(2)}, u32[]{:S(2)}) collective-permute-start(bf16[1,48,256]{2,1,0:T(8,128)(2,1)S(1)} %get-tuple-element.32), channel_id=1, source_target_pairs={{0,32},{32,64},{64,96},{1,33},{33,65},{65,97},{2,34},{34,66},{66,9... | collective-permute-start | bytes 73736 | tf_op jit(solution)/shard_map/ppermute | solution.py:24
  107.3 1.3 %collective-permute-start.7 = (bf16[1,48,256]{2,1,0:T(8,128)(2,1)S(1)}, bf16[1,48,256]{2,1,0:T(8,128)(2,1)S(1)}, u32[]{:S(2)}, u32[]{:S(2)}) collective-permute-start(bf16[1,48,256]{2,1,0:T(8,128)(2,1)S(1)} %get-tuple-element.31), channel_id=1, source_target_pairs={{32,0},{64,32},{96,64},{33,1},{65,33},{97,65},{34,2},{66,34},{98,6... | collective-permute-start | bytes 73736 | tf_op jit(solution)/shard_map/ppermute | solution.py:26
  108.6 0.2 collective-permute-done.6
  108.8 4.2 %collective-permute-done.7 = bf16[1,48,256]{2,1,0:T(8,128)(2,1)S(1)} collective-permute-done((bf16[1,48,256]{2,1,0:T(8,128)(2,1)S(1)}, bf16[1,48,256]{2,1,0:T(8,128)(2,1)S(1)}, u32[]{:S(2)}, u32[]{:S(2)}) %collective-permute-start.7) | collective-permute-done | bytes 24608 | tf_op jit(solution)/shard_map/ppermute | solution.py:26
  113.0 0.0 collective-permute-done.5
  113.0 0.0 copy-start.7
  113.1 0.1 pad_maximum_fusion.2
  113.2 0.1 collective-permute-start.8
  113.3 5.1 %collective-permute-start.9 = (bf16[26,1,256]{2,1,0:T(2,128)(2,1)S(1)}, bf16[26,1,256]{2,1,0:T(2,128)(2,1)S(1)}, u32[]{:S(2)}, u32[]{:S(2)}) collective-permute-start(bf16[26,1,256]{2,1,0:T(2,128)(2,1)S(1)} %get-tuple-element.23), channel_id=1, source_target_pairs={{1,0},{2,1},{3,2},{4,3},{5,4},{6,5},{7,6},{8,7},{9,8},{10,9},{11,1... | collective-permute-start | bytes 39944 | tf_op jit(solution)/shard_map/ppermute | solution.py:26
  118.3 0.0 copy-done.7
  118.3 0.3 fusion.9
  118.7 1.2 collective-permute-done.8
  119.9 0.0 collective-permute-done.9
  119.9 0.5 pad_maximum_fusion.1
  120.4 0.1 fusion.42
  120.5 0.3 fusion.41
  120.8 0.3 convolution_add_fusion.7
  121.1 0.3 convolution_add_fusion.6
  121.4 0.3 convolution_add_fusion.5
  121.8 0.5 convolution_add_fusion.4
  122.2 0.3 convolution_add_fusion.3
  122.5 0.3 convolution_add_fusion.2
  122.9 0.3 convolution_add_fusion.1
  123.2 0.3 convolution_add_fusion
  123.5 1.0 add_convert_fusion
  (11 shorter events, 0.1 us)
Async XLA Ops:
  0.0 26.6 %copy-start.5 = (f32[256]{0:T(256)S(1)}, f32[256]{0:T(256)}, u32[]{:S(2)}) copy-start(f32[256]{0:T(256)} %param.13) | copy-start | bytes 3076
  0.0 1.4 %copy-start = (f32[12288,32]{0,1:T(8,128)S(1)}, f32[12288,32]{0,1:T(8,128)}, u32[]{:S(2)}) copy-start(f32[12288,32]{0,1:T(8,128)} %param.9) | copy-start | bytes 4718596
  1.4 0.8 copy-start.2
  2.2 0.8 copy-start.3
  3.0 23.6 %copy-start.1 = (bf16[256,256]{1,0:T(8,128)(2,1)S(1)}, bf16[256,256]{1,0:T(8,128)(2,1)}, u32[]{:S(2)}) copy-start(bf16[256,256]{1,0:T(8,128)(2,1)} %second_ref.1) | copy-start | bytes 393220
  3.0 23.6 %copy-start.4 = (f32[32,256]{1,0:T(8,128)S(1)}, f32[32,256]{1,0:T(8,128)}, u32[]{:S(2)}) copy-start(f32[32,256]{1,0:T(8,128)} %first_ref.1) | copy-start | bytes 98308
  81.4 9.4 %collective-permute-start = (bf16[2,48,256]{2,1,0:T(8,128)(2,1)S(1)}, bf16[2,48,256]{2,1,0:T(8,128)(2,1)S(1)}, u32[]{:S(2)}, u32[]{:S(2)}) collective-permute-start(bf16[2,48,256]{2,1,0:T(8,128)(2,1)S(1)} %pad_maximum_fusion.6), channel_id=1, source_target_pairs={{0,16},{1,17},{2,18},{3,19},{4,20},{5,21},{6,22},{7,23},{8,24},{9,... | collective-permute-start | bytes 147464 | tf_op jit(solution)/shard_map/ppermute | solution.py:35
  82.0 4.5 %collective-permute-start.1 = (bf16[1,48,256]{2,1,0:T(8,128)(2,1)S(1)}, bf16[1,48,256]{2,1,0:T(8,128)(2,1)S(1)}, u32[]{:S(2)}, u32[]{:S(2)}) collective-permute-start(bf16[1,48,256]{2,1,0:T(8,128)(2,1)S(1)} %get-tuple-element.36), channel_id=1, source_target_pairs={{0,32},{32,64},{64,96},{1,33},{33,65},{65,97},{2,34},{34,66},{66,9... | collective-permute-start | bytes 73736 | tf_op jit(solution)/shard_map/ppermute | solution.py:24
  85.0 5.7 %collective-permute-start.2 = (bf16[1,48,256]{2,1,0:T(8,128)(2,1)S(1)}, bf16[1,48,256]{2,1,0:T(8,128)(2,1)S(1)}, u32[]{:S(2)}, u32[]{:S(2)}) collective-permute-start(bf16[1,48,256]{2,1,0:T(8,128)(2,1)S(1)} %get-tuple-element.35), channel_id=1, source_target_pairs={{32,0},{64,32},{96,64},{33,1},{65,33},{97,65},{34,2},{66,34},{98,6... | collective-permute-start | bytes 73736 | tf_op jit(solution)/shard_map/ppermute | solution.py:26
  90.7 7.2 %copy-start.6 = (bf16[3,3,256,256]{3,2,1,0:T(8,128)(2,1)S(1)}, bf16[3,3,256,256]{3,2,1,0:T(8,128)(2,1)}, u32[]{:S(2)}) copy-start(bf16[3,3,256,256]{3,2,1,0:T(8,128)(2,1)} %param.15) | copy-start | bytes 3538948
  90.9 8.5 %collective-permute-start.3 = (bf16[26,1,256]{2,1,0:T(2,128)(2,1)S(1)}, bf16[26,1,256]{2,1,0:T(2,128)(2,1)S(1)}, u32[]{:S(2)}, u32[]{:S(2)}) collective-permute-start(bf16[26,1,256]{2,1,0:T(2,128)(2,1)S(1)} %get-tuple-element.28), channel_id=1, source_target_pairs={{0,1},{1,2},{2,3},{3,4},{4,5},{5,6},{6,7},{7,8},{8,9},{9,10},{10,1... | collective-permute-start | bytes 39944 | tf_op jit(solution)/shard_map/ppermute | solution.py:24
  95.0 4.4 %collective-permute-start.4 = (bf16[26,1,256]{2,1,0:T(2,128)(2,1)S(1)}, bf16[26,1,256]{2,1,0:T(2,128)(2,1)S(1)}, u32[]{:S(2)}, u32[]{:S(2)}) collective-permute-start(bf16[26,1,256]{2,1,0:T(2,128)(2,1)S(1)} %get-tuple-element.27), channel_id=1, source_target_pairs={{1,0},{2,1},{3,2},{4,3},{5,4},{6,5},{7,6},{8,7},{9,8},{10,9},{11,1... | collective-permute-start | bytes 39944 | tf_op jit(solution)/shard_map/ppermute | solution.py:26
  102.5 0.7 copy-start.8
  103.6 9.4 %collective-permute-start.5 = (bf16[2,48,256]{2,1,0:T(8,128)(2,1)S(1)}, bf16[2,48,256]{2,1,0:T(8,128)(2,1)S(1)}, u32[]{:S(2)}, u32[]{:S(2)}) collective-permute-start(bf16[2,48,256]{2,1,0:T(8,128)(2,1)S(1)} %pad_maximum_fusion.7), channel_id=1, source_target_pairs={{0,16},{1,17},{2,18},{3,19},{4,20},{5,21},{6,22},{7,23},{8,24},{9,... | collective-permute-start | bytes 147464 | tf_op jit(solution)/shard_map/ppermute | solution.py:35
  103.7 5.1 %collective-permute-start.6 = (bf16[1,48,256]{2,1,0:T(8,128)(2,1)S(1)}, bf16[1,48,256]{2,1,0:T(8,128)(2,1)S(1)}, u32[]{:S(2)}, u32[]{:S(2)}) collective-permute-start(bf16[1,48,256]{2,1,0:T(8,128)(2,1)S(1)} %get-tuple-element.32), channel_id=1, source_target_pairs={{0,32},{32,64},{64,96},{1,33},{33,65},{65,97},{2,34},{34,66},{66,9... | collective-permute-start | bytes 73736 | tf_op jit(solution)/shard_map/ppermute | solution.py:24
  107.3 5.7 %collective-permute-start.7 = (bf16[1,48,256]{2,1,0:T(8,128)(2,1)S(1)}, bf16[1,48,256]{2,1,0:T(8,128)(2,1)S(1)}, u32[]{:S(2)}, u32[]{:S(2)}) collective-permute-start(bf16[1,48,256]{2,1,0:T(8,128)(2,1)S(1)} %get-tuple-element.31), channel_id=1, source_target_pairs={{32,0},{64,32},{96,64},{33,1},{65,33},{97,65},{34,2},{66,34},{98,6... | collective-permute-start | bytes 73736 | tf_op jit(solution)/shard_map/ppermute | solution.py:26
  113.0 5.3 %copy-start.7 = (bf16[3,3,256,256]{3,2,1,0:T(8,128)(2,1)S(1)}, bf16[3,3,256,256]{3,2,1,0:T(8,128)(2,1)}, u32[]{:S(2)}) copy-start(bf16[3,3,256,256]{3,2,1,0:T(8,128)(2,1)} %param.17) | copy-start | bytes 3538948
  113.2 6.7 %collective-permute-start.8 = (bf16[26,1,256]{2,1,0:T(2,128)(2,1)S(1)}, bf16[26,1,256]{2,1,0:T(2,128)(2,1)S(1)}, u32[]{:S(2)}, u32[]{:S(2)}) collective-permute-start(bf16[26,1,256]{2,1,0:T(2,128)(2,1)S(1)} %get-tuple-element.24), channel_id=1, source_target_pairs={{0,1},{1,2},{2,3},{3,4},{4,5},{5,6},{6,7},{7,8},{8,9},{9,10},{10,1... | collective-permute-start | bytes 39944 | tf_op jit(solution)/shard_map/ppermute | solution.py:24
  113.3 6.6 %collective-permute-start.9 = (bf16[26,1,256]{2,1,0:T(2,128)(2,1)S(1)}, bf16[26,1,256]{2,1,0:T(2,128)(2,1)S(1)}, u32[]{:S(2)}, u32[]{:S(2)}) collective-permute-start(bf16[26,1,256]{2,1,0:T(2,128)(2,1)S(1)} %get-tuple-element.23), channel_id=1, source_target_pairs={{1,0},{2,1},{3,2},{4,3},{5,4},{6,5},{7,6},{8,7},{9,8},{10,9},{11,1... | collective-permute-start | bytes 39944 | tf_op jit(solution)/shard_map/ppermute | solution.py:26
where the time goes:
time: 125 us; the launch traced here: 124 us
  Pallas kernels  78.3 us (63%)
  starting transfers between devices  22 us (18%)
  waiting for transfers between devices  11.3 us (9%)
  matrix products  5.77 us (5%)
  local copies, waits for them, and re-layouts  4.21 us (3%)
  other arithmetic  2.58 us (2%)
    pallas_call x1, Pallas kernels, exchange(): pl.pallas_call(functools.partial(exchange_kernel, bands, sector_dims, gro...  54.7 us
    pallas_call x1, Pallas kernels, dispatch(): pl.pallas_call(functools.partial(dispatch_kernel, shards, capacity, unrol...  23.6 us
    ppermute x4, starting transfers between devices, with_halo(): lax.ppermute(tail, axis, [(i, (i + 1) % count) for i in range(ends)])  10.8 us
    ppermute x4, starting transfers between devices, with_halo(): lax.ppermute(head, axis, [((i + 1) % count, i) for i in range(ends)])  10.5 us
    ppermute x4, waiting for transfers between devices, with_halo(): lax.ppermute(head, axis, [((i + 1) % count, i) for i in range(ends)])  8.54 us
    dot_general x18, matrix products, convolve(): jnp.dot(window, kernel[row_tap, col_tap], preferred_element_type=jnp.floa...  5.77 us
    unnamed x18, local copies, waits for them, and re-layouts  3.4 us
    ppermute x4, waiting for transfers between devices, with_halo(): lax.ppermute(tail, axis, [(i, (i + 1) % count) for i in range(ends)])  2.74 us
  transfers between devices with their start and end apart: 10, of which 7 were waited for; matrix products, arithmetic and copies ran while one was open for 1% of the time, Pallas kernels for 0%

commit v1 on v0

--- a/solution.py
+++ b/solution.py
@@ -11,52 +11,6 @@
 TILE_ROWS = 24
 TILE_COLS = 48
 BLOCK = 256
-
-
-def with_halo(cells, sides, width, closed):
-    for axis, dim in sides:
-        count = lax.axis_size(axis)
-        ends = count if closed else count - 1
-        head = lax.slice_in_dim(cells, 0, width, axis=dim)
-        tail = lax.slice_in_dim(cells, cells.shape[dim] - width, cells.shape[dim], axis=dim)
-        cells = jnp.concatenate(
-            [
-                lax.ppermute(tail, axis, [(i, (i + 1) % count) for i in range(ends)]),
-                cells,
-                lax.ppermute(head, axis, [((i + 1) % count, i) for i in range(ends)]),
-            ],
-            axis=dim,
-        )
-    return cells
-
-
-def shifted(shard, axis, by):
-    count = lax.axis_size(axis)
-    return lax.ppermute(shard, axis, [(i, (i + by) % count) for i in range(count)])
-
-
-def convolve(tile, kernel):
-    padded = with_halo(tile, (("lat", 0),), 1, False)
-    edges = jnp.stack([tile[0], tile[-1]])
-    partner = shifted(edges, "lon", lax.axis_size("lon") // 2)
-    band = lax.axis_index("lat")
-    upper = jnp.where(band == 0, partner[0], padded[0])
-    lower = jnp.where(band == lax.axis_size("lat") - 1, partner[1], padded[-1])
-    padded = jnp.concatenate([upper[None], tile, lower[None]], axis=0)
-    padded = with_halo(padded, (("lon", 1),), 1, True)
-    tile_rows = tile.shape[0]
-    tile_cols = tile.shape[1]
-    width = tile.shape[2]
-    total = jnp.zeros((tile_rows * tile_cols, kernel.shape[3]), jnp.float32)
-    for row_tap in range(3):
-        for col_tap in range(3):
-            window = padded[row_tap : row_tap + tile_rows, col_tap : col_tap + tile_cols].reshape(
-                -1, width
-            )
-            total = total + jnp.dot(
-                window, kernel[row_tap, col_tap], preferred_element_type=jnp.float32
-            )
-    return total.reshape(tile_rows, tile_cols, -1)
 
 
 def dispatch_kernel(shards, capacity, unroll, obs_ref, dest_ref, cell_ref, rows_ref, cells_ref,
@@ -176,6 +130,124 @@
     )(obs.T, dest.reshape(1, -1), cells.reshape(1, -1))
 
 
+PITCH = 64
+
+
+def encode_tile(sums, scale, first_kernel, second_kernel, bias_ref, out_ref, field, shifted, middle,
+                row_edges, column_edges, corner_edges, row_halos, column_halos, corner_halos,
+                send_halo, recv_halo):
+    f32, bf16, i32 = jnp.float32, jnp.bfloat16, jnp.int32
+    mesh_id = pl.DeviceIdType.MESH
+    bands, sectors = lax.axis_size("lat"), lax.axis_size("lon")
+    band, sector = lax.axis_index("lat"), lax.axis_index("lon")
+    width = sums.shape[1]
+
+    def at(line, column):
+        return (line + 3) * PITCH + column
+
+    for line in range(TILE_ROWS):
+        block = sums[pl.ds(line * TILE_COLS, TILE_COLS), :] * scale[:, line:line + 1]
+        block = block.astype(bf16)
+        field[pl.ds(at(line, 0), TILE_COLS), :] = block.astype(f32)
+        if line < 2:
+            row_edges[0, line] = block
+        if line >= TILE_ROWS - 2:
+            row_edges[1, TILE_ROWS - 1 - line] = block
+    for side, columns in enumerate(((0, 1), (TILE_COLS - 1, TILE_COLS - 2))):
+        for depth, column in enumerate(columns):
+            for line in range(TILE_ROWS):
+                column_edges[side, depth, pl.ds(line, 1), :] = field[pl.ds(at(line, column), 1), :]
+        for end, lines in enumerate(((0, 1), (TILE_ROWS - 1, TILE_ROWS - 2))):
+            for i, line in enumerate(lines):
+                for j, column in enumerate(columns):
+                    corner_edges[end, side, pl.ds(2 * i + j, 1), :] = field[pl.ds(at(line, column), 1), :]
+
+    north = band > 0
+    south = band < bands - 1
+    vertical = (
+        (jnp.where(north, band - 1, 0), jnp.where(north, 0, sectors // 2), jnp.where(north, 1, 0)),
+        (jnp.where(south, band + 1, bands - 1), jnp.where(south, 0, sectors // 2), jnp.where(south, 0, 1)),
+    )
+    copies = []
+
+    def ship(source, target, slot, target_band, shift):
+        copies.append(
+            pltpu.make_async_remote_copy(
+                src_ref=source, dst_ref=target, send_sem=send_halo.at[len(copies)], recv_sem=recv_halo.at[slot],
+                device_id=(target_band, lax.rem(sector + shift + 2 * sectors, sectors)), device_id_type=mesh_id))
+        copies[-1].start()
+
+    for end, (target_band, shift, landing) in enumerate(vertical):
+        ship(row_edges.at[end], row_halos.at[landing], landing, target_band, shift)
+    for side, step in enumerate((-1, 1)):
+        ship(column_edges.at[side], column_halos.at[1 - side], 2 + 1 - side, band, step)
+    for end, (target_band, shift, landing) in enumerate(vertical):
+        for side, step in enumerate((-1, 1)):
+            ship(corner_edges.at[end, side], corner_halos.at[landing, 1 - side], 4 + 2 * landing + 1 - side,
+                 target_band, shift + step)
+    arrivals = [row_halos.at[0], row_halos.at[1], column_halos.at[0], column_halos.at[1]]
+    arrivals += [corner_halos.at[end, side] for end in range(2) for side in range(2)]
+    for slot, buffer in enumerate(arrivals):
+        pltpu.make_async_remote_copy(
+            src_ref=buffer, dst_ref=buffer, send_sem=send_halo.at[slot], recv_sem=recv_halo.at[slot],
+            device_id=(band, sector), device_id_type=mesh_id).wait_recv()
+
+    for end, lines in enumerate(((-1, -2), (TILE_ROWS, TILE_ROWS + 1))):
+        for depth, line in enumerate(lines):
+            field[pl.ds(at(line, 0), TILE_COLS), :] = row_halos[end, depth].astype(f32)
+    for side, columns in enumerate(((-1, -2), (TILE_COLS, TILE_COLS + 1))):
+        for depth, column in enumerate(columns):
+            for line in range(TILE_ROWS):
+                field[pl.ds(at(line, column), 1), :] = column_halos[side, depth, pl.ds(line, 1), :]
+        for end, lines in enumerate(((-1, -2), (TILE_ROWS, TILE_ROWS + 1))):
+            for i, line in enumerate(lines):
+                for j, column in enumerate(columns):
+                    field[pl.ds(at(line, column), 1), :] = corner_halos[end, side, pl.ds(2 * i + j, 1), :]
+
+    def spread(array, start, stop):
+        for tap in range(3):
+            shifted[pl.ds(start, stop - start), tap * width:(tap + 1) * width] = (
+                array[pl.ds(start + tap - 1, stop - start), :].astype(bf16))
+
+    low, high = at(-1, -16), at(TILE_ROWS, PITCH)
+    spread(field, low - PITCH, high + PITCH)
+    total = 0.0
+    for tap in range(3):
+        total += jnp.dot(shifted[pl.ds(low + (tap - 1) * PITCH, high - low), :], first_kernel[tap],
+                         preferred_element_type=f32)
+    tall = PITCH + 16
+    turned = 0.0
+    for tap in range(3):
+        lines = jnp.concatenate(
+            [shifted[pl.ds(at(line - (tap - 1), -16), tall), :] for line in (-1, TILE_ROWS)], axis=0)
+        turned += jnp.dot(lines, first_kernel[tap], preferred_element_type=f32)
+    half_bias = 0.5 * bias_ref[...]
+
+    def activate(value):
+        half = 0.5 * value + half_bias
+        return half + half * jnp.tanh(half)
+
+    middle[pl.ds(low, high - low), :] = activate(total)
+    turned = activate(turned)
+    spot = lax.broadcasted_iota(i32, (tall, width), 0)
+    inside = (spot >= 15) & (spot < 16 + TILE_COLS + 1)
+    for index, (line, polar) in enumerate(((-1, band == 0), (TILE_ROWS, band == bands - 1))):
+        place = pl.ds(at(line, -16), tall)
+        chosen = jnp.where(polar, 1, 0)
+        middle[place, :] = jnp.where(
+            inside & (chosen == 1), turned[index * tall:(index + 1) * tall], middle[place, :])
+
+    start, stop = at(0, 0), at(TILE_ROWS, 0)
+    spread(middle, start - PITCH, stop + PITCH)
+    total = field[pl.ds(start, stop - start), :]
+    for tap in range(3):
+        total += jnp.dot(shifted[pl.ds(start + (tap - 1) * PITCH, stop - start), :], second_kernel[tap],
+                         preferred_element_type=f32)
+    out_ref[...] = total.reshape(TILE_ROWS, PITCH, width)[:, :TILE_COLS].astype(bf16)
+    for copy in copies:
+        copy.wait_send()
+
+
 def place_of(step, bands, sector_dims):
     digits = []
     for size in reversed(sector_dims):
@@ -194,8 +266,11 @@
     return band, sector
 
 
-def exchange_kernel(bands, sector_dims, group, chunk, rows_ref, cells_ref, first_ref, bias_ref, second_ref, latent_ref,
-                    rows_got, cells_got, features, sums, counts, own_sem, send_rows, send_cells, recv_rows, recv_cells):
+def exchange_kernel(bands, sector_dims, group, chunk, rows_ref, cells_ref, first_ref, bias_ref, second_ref,
+                    conv_first_ref, conv_bias_ref, conv_second_ref, out_ref,
+                    rows_got, cells_got, features, sums, counts, first_kernel, second_kernel, field, shifted, middle,
+                    row_edges, column_edges, corner_edges, row_halos, column_halos, corner_halos, own_sem, send_rows, send_cells, recv_rows, recv_cells,
+                    send_halo, recv_halo):
     shards, packed, _ = rows_got.shape
     values = first_ref.shape[0]
     width = second_ref.shape[1]
@@ -237,6 +312,12 @@
     own_cells = pltpu.make_async_copy(cells_ref.at[me], cells_got.at[0], own_sem.at[1])
     own_rows.start()
     own_cells.start()
+    kernels = [
+        pltpu.make_async_copy(conv_first_ref, first_kernel, own_sem.at[2]),
+        pltpu.make_async_copy(conv_second_ref, second_kernel, own_sem.at[3]),
+    ]
+    for copy in kernels:
+        copy.start()
     lax.fori_loop(1, shards, send, 0)
 
     sums[...] = jnp.zeros_like(sums)
@@ -295,9 +376,10 @@
     lax.fori_loop(0, shards // group, work, 0)
 
     scale = 1.0 / jnp.maximum(counts[...], 1.0)
-    for line in range(TILE_ROWS):
-        block = sums[pl.ds(line * TILE_COLS, TILE_COLS), :] * scale[:, line:line + 1]
-        latent_ref[line] = block.astype(bf16)
+    for copy in kernels:
+        copy.wait()
+    encode_tile(sums, scale, first_kernel, second_kernel, conv_bias_ref, out_ref, field, shifted, middle,
+                row_edges, column_edges, corner_edges, row_halos, column_halos, corner_halos, send_halo, recv_halo)
 
     def drain(step, _):
         for copy in copies(step):
@@ -307,17 +389,18 @@
     lax.fori_loop(1, shards, drain, 0)
 
 
-def exchange(rows, cells, first_weight, first_bias, second_weight, bands, sector_dims, group=16, chunk=4):
+def exchange(rows, cells, first_weight, first_bias, second_weight, conv_first, conv_bias, conv_second, bands, sector_dims, group=16, chunk=4):
     shards, packed, _ = rows.shape
     width = second_weight.shape[1]
     vmem = pl.BlockSpec(memory_space=pltpu.VMEM)
     anywhere = pl.BlockSpec(memory_space=pl.ANY)
     packing = 128 // first_weight.shape[0]
     dma = pltpu.SemaphoreType.DMA
+    field_rows = (TILE_ROWS + 5) * PITCH + 16
     return pl.pallas_call(
         functools.partial(exchange_kernel, bands, sector_dims, group, chunk),
         out_shape=jax.ShapeDtypeStruct((TILE_ROWS, TILE_COLS, width), jnp.bfloat16),
-        in_specs=[anywhere, anywhere, vmem, vmem, vmem],
+        in_specs=[anywhere, anywhere, vmem, vmem, vmem, anywhere, vmem, anywhere],
         out_specs=vmem,
         scratch_shapes=[
             pltpu.VMEM((shards, packed, 128), jnp.bfloat16),
@@ -325,12 +408,25 @@
             pltpu.VMEM((group, packing, packed, width), jnp.bfloat16),
             pltpu.VMEM((TILE_ROWS * TILE_COLS, width), jnp.float32),
             pltpu.VMEM((TILE_COLS, 32), jnp.float32),
-            dma((2,)), dma((shards,)), dma((shards,)), dma((shards,)), dma((shards,)),
+            pltpu.VMEM((3, 3 * width, width), jnp.bfloat16),
+            pltpu.VMEM((3, 3 * width, width), jnp.bfloat16),
+            pltpu.VMEM((field_rows, width), jnp.float32),
+            pltpu.VMEM((field_rows, 3 * width), jnp.bfloat16),
+            pltpu.VMEM((field_rows, width), jnp.float32),
+            pltpu.VMEM((2, 2, TILE_COLS, width), jnp.bfloat16),
+            pltpu.VMEM((2, 2, TILE_ROWS, width), jnp.float32),
+            pltpu.VMEM((2, 2, 8, width), jnp.float32),
+            pltpu.VMEM((2, 2, TILE_COLS, width), jnp.bfloat16),
+            pltpu.VMEM((2, 2, TILE_ROWS, width), jnp.float32),
+            pltpu.VMEM((2, 2, 8, width), jnp.float32),
+            dma((4,)), dma((shards,)), dma((shards,)), dma((shards,)), dma((shards,)),
+            dma((8,)), dma((8,)),
         ],
         compiler_params=pltpu.CompilerParams(
             collective_id=0, has_side_effects=True, vmem_limit_bytes=48 * 1024 * 1024),
         name="exchange",
-    )(rows, cells, first_weight, first_bias.reshape(1, -1), second_weight)
+    )(rows, cells, first_weight, first_bias.reshape(1, -1), second_weight,
+      conv_first.reshape(3, 3 * width, width), conv_bias.reshape(1, -1), conv_second.reshape(3, 3 * width, width))
 
 
 def body(
@@ -349,9 +445,8 @@
     shards = bands * sectors
     capacity = 2 * observations.shape[0] // shards
     rows, spots = dispatch(observations, destinations, cells, shards, capacity)
-    latent = exchange(rows, spots, first_weight, first_bias, second_weight, bands, (4, 4, 2))
-    middle = jax.nn.silu(convolve(latent, conv_first) + conv_bias).astype(jnp.bfloat16)
-    return (latent.astype(jnp.float32) + convolve(middle, conv_second)).astype(jnp.bfloat16)
+    return exchange(rows, spots, first_weight, first_bias, second_weight, conv_first, conv_bias, conv_second,
+                    bands, (4, 4, 2))
 
 
 def solution(mesh):

time: 125 us -> 101 us (0.81)
  starting transfers between devices: 22 us -> 0 us
  Pallas kernels: 78.3 us -> 95.3 us
  waiting for transfers between devices: 11.3 us -> 0 us
  matrix products: 5.77 us -> 0 us
  other arithmetic: 2.58 us -> 0 us
    ppermute x10 -> x0, starting transfers between devices: 22 us -> none  [the longest x4 10.8 us: with_halo(): lax.ppermute(tail, axis, [(i, (i + 1) % count) for i in range(ends)])]
    pallas_call x1, Pallas kernels: 54.7 us -> 71.8 us  [exchange(): pl.pallas_call(functools.partial(exchange_kernel, bands, sector_dims, gro...]
    ppermute x10 -> x0, waiting for transfers between devices: 11.3 us -> none  [the longest x4 8.54 us: with_halo(): lax.ppermute(head, axis, [((i + 1) % count, i) for i in range(ends)])]
    dot_general x18 -> x0, matrix products: 5.77 us -> none  [convolve(): jnp.dot(window, kernel[row_tap, col_tap], preferred_element_type=jnp.floa...]
    unnamed x18 -> x19, local copies, waits for them, and re-layouts: 3.4 us -> 5.13 us
    convert_element_type x2 -> x0, other arithmetic: 1.3 us -> none  [the longest x1 0.98 us: body(): (latent.astype(jnp.float32) + convolve(middle, conv_second)).astype(jnp.b...]
  transfers between devices with their start and end apart: 10 -> 0, of which waited for: 7 -> 0; matrix products, arithmetic and copies ran while one was open for 1% -> 0% of each run, Pallas kernels for 0% -> 0%
where the time goes in v1:
time: 101 us
  Pallas kernels  95.3 us (94%)
  local copies, waits for them, and re-layouts  5.13 us (5%)
    pallas_call x1, Pallas kernels, exchange(): pl.pallas_call(functools.partial(exchange_kernel, bands, sector_dims, gro...  71.8 us
    pallas_call x1, Pallas kernels, dispatch(): pl.pallas_call(functools.partial(dispatch_kernel, shards, capacity, unrol...  23.6 us
    unnamed x19, local copies, waits for them, and re-layouts  5.13 us

profile of v1, /device:TPU:0, one launch (start us, length us, event | category | flops | bytes accessed | tf_op | source)
XLA Modules:
  0.0 100.5 jit_solution(3722730587410983859)
XLA Ops:
  0.0 0.0 copy-start.8
  0.0 0.0 copy-start.7
  0.0 0.0 copy-start
  0.0 1.4 %copy-done = f32[12288,32]{0,1:T(8,128)S(1)} copy-done((f32[12288,32]{0,1:T(8,128)S(1)}, f32[12288,32]{0,1:T(8,128)}, u32[]{:S(2)}) %copy-start) | copy-done | bytes 1572888
  1.4 0.0 copy-start.4
  1.4 0.8 copy-done.4
  2.2 0.0 copy-start.5
  2.2 0.8 copy-done.5
  3.0 0.0 copy-start.1
  3.0 0.0 copy-start.3
  3.0 0.0 copy-start.6
  3.0 23.6 %dispatch.1 = (bf16[128,48,128]{2,1,0:T(8,128)(2,1)S(1)}, s32[128,2,128]{2,1,0:T(2,128)S(1)}) custom-call(f32[32,12288]{1,0:T(8,128)S(1)} %bitcast.7, s32[1,12288]{1,0:T(1,128)S(1)} %bitcast.10, s32[1,12288]{1,0:T(1,128)S(1)} %bitcast.11), custom_call_target="tpu_custom_call" | custom-call | tf_op jit(solution)/shard_map/dispatch/pallas_call | solution.py:112
  26.6 0.0 copy-done.8
  26.6 0.0 copy-done.7
  26.6 0.0 copy-done.1
  26.6 0.0 copy-done.3
  26.7 0.0 copy-done.6
  26.7 0.0 copy-start.2
  26.7 1.3 %copy-done.2 = bf16[3,3,256,256]{3,2,1,0:T(8,128)(2,1)S(1)} copy-done((bf16[3,3,256,256]{3,2,1,0:T(8,128)(2,1)S(1)}, bf16[3,3,256,256]{3,2,1,0:T(8,128)(2,1)}, u32[]{:S(2)}) %copy-start.2) | copy-done | bytes 1179672
  27.9 71.8 %exchange.1 = bf16[24,48,256]{2,1,0:T(8,128)(2,1)S(1)} custom-call(bf16[128,48,128]{2,1,0:T(8,128)(2,1)S(1)} %get-tuple-element.7.rows_ref, s32[128,2,128]{2,1,0:T(2,128)S(1)} %get-tuple-element.8.cells_ref, f32[32,256]{1,0:T(8,128)S(1)} %copy-done.6, f32[1,256]{1,0:T(1,128)S(1)} %bitcast.12, bf16[256,256]{1,0:T(8,128)(2,1)S(1)} %copy-done.3, ...), custom_call_target="tpu_custom_call" | custom-call | tf_op jit(solution)/shard_map/exchange/pallas_call | solution.py:400
  99.7 0.8 copy.11
Async XLA Ops:
  0.0 26.6 %copy-start.8 = (f32[256]{0:T(256)S(1)}, f32[256]{0:T(256)}, u32[]{:S(2)}) copy-start(f32[256]{0:T(256)} %param.16) | copy-start | bytes 3076
  0.0 26.6 %copy-start.7 = (f32[256]{0:T(256)S(1)}, f32[256]{0:T(256)}, u32[]{:S(2)}) copy-start(f32[256]{0:T(256)} %param.13) | copy-start | bytes 3076
  0.0 1.4 %copy-start = (f32[12288,32]{0,1:T(8,128)S(1)}, f32[12288,32]{0,1:T(8,128)}, u32[]{:S(2)}) copy-start(f32[12288,32]{0,1:T(8,128)} %param.9) | copy-start | bytes 4718596
  1.4 0.8 copy-start.4
  2.2 0.8 copy-start.5
  3.0 23.6 %copy-start.1 = (bf16[3,3,256,256]{3,2,1,0:T(8,128)(2,1)S(1)}, bf16[3,3,256,256]{3,2,1,0:T(8,128)(2,1)}, u32[]{:S(2)}) copy-start(bf16[3,3,256,256]{3,2,1,0:T(8,128)(2,1)} %param.15) | copy-start | bytes 3538948
  3.0 23.6 %copy-start.3 = (bf16[256,256]{1,0:T(8,128)(2,1)S(1)}, bf16[256,256]{1,0:T(8,128)(2,1)}, u32[]{:S(2)}) copy-start(bf16[256,256]{1,0:T(8,128)(2,1)} %second_ref.1) | copy-start | bytes 393220
  3.0 23.6 %copy-start.6 = (f32[32,256]{1,0:T(8,128)S(1)}, f32[32,256]{1,0:T(8,128)}, u32[]{:S(2)}) copy-start(f32[32,256]{1,0:T(8,128)} %first_ref.1) | copy-start | bytes 98308
  26.7 1.3 %copy-start.2 = (bf16[3,3,256,256]{3,2,1,0:T(8,128)(2,1)S(1)}, bf16[3,3,256,256]{3,2,1,0:T(8,128)(2,1)}, u32[]{:S(2)}) copy-start(bf16[3,3,256,256]{3,2,1,0:T(8,128)(2,1)} %param.17) | copy-start | bytes 3538948

commit v2 on v1

v2 whole, which is shorter than its diff:
```python
import functools

import jax
import jax.numpy as jnp
from jax import lax
from jax.experimental import pallas as pl
from jax.experimental.pallas import tpu as pltpu
from jax.sharding import PartitionSpec as P

TILE_ROWS = 24
TILE_COLS = 48
BLOCK = 256
ROOM = 16384


PITCH = 64


def encode_tile(sums, scale, first_kernel, second_kernel, bias_ref, out_ref, field, shifted, middle,
                row_edges, column_edges, corner_edges, row_halos, column_halos, corner_halos,
                send_halo, recv_halo):
    f32, bf16, i32 = jnp.float32, jnp.bfloat16, jnp.int32
    mesh_id = pl.DeviceIdType.MESH
    bands, sectors = lax.axis_size("lat"), lax.axis_size("lon")
    band, sector = lax.axis_index("lat"), lax.axis_index("lon")
    width = sums.shape[1]

    def at(line, column):
        return (line + 3) * PITCH + column

    for line in range(TILE_ROWS):
        block = sums[pl.ds(line * TILE_COLS, TILE_COLS), :] * scale[:, line:line + 1]
        block = block.astype(bf16)
        field[pl.ds(at(line, 0), TILE_COLS), :] = block.astype(f32)
        if line < 2:
            row_edges[0, line] = block
        if line >= TILE_ROWS - 2:
            row_edges[1, TILE_ROWS - 1 - line] = block
    for side, columns in enumerate(((0, 1), (TILE_COLS - 1, TILE_COLS - 2))):
        for depth, column in enumerate(columns):
            for line in range(TILE_ROWS):
                column_edges[side, depth, pl.ds(line, 1), :] = field[pl.ds(at(line, column), 1), :]
        for end, lines in enumerate(((0, 1), (TILE_ROWS - 1, TILE_ROWS - 2))):
            for i, line in enumerate(lines):
                for j, column in enumerate(columns):
                    corner_edges[end, side, pl.ds(2 * i + j, 1), :] = field[pl.ds(at(line, column), 1), :]

    north = band > 0
    south = band < bands - 1
    vertical = (
        (jnp.where(north, band - 1, 0), jnp.where(north, 0, sectors // 2), jnp.where(north, 1, 0)),
        (jnp.where(south, band + 1, bands - 1), jnp.where(south, 0, sectors // 2), jnp.where(south, 0, 1)),
    )
    copies = []

    def ship(source, target, slot, target_band, shift):
        copies.append(
            pltpu.make_async_remote_copy(
                src_ref=source, dst_ref=target, send_sem=send_halo.at[len(copies)], recv_sem=recv_halo.at[slot],
                device_id=(target_band, lax.rem(sector + shift + 2 * sectors, sectors)), device_id_type=mesh_id))
        copies[-1].start()

    for end, (target_band, shift, landing) in enumerate(vertical):
        ship(row_edges.at[end], row_halos.at[landing], landing, target_band, shift)
    for side, step in enumerate((-1, 1)):
        ship(column_edges.at[side], column_halos.at[1 - side], 2 + 1 - side, band, step)
    for end, (target_band, shift, landing) in enumerate(vertical):
        for side, step in enumerate((-1, 1)):
            ship(corner_edges.at[end, side], corner_halos.at[landing, 1 - side], 4 + 2 * landing + 1 - side,
                 target_band, shift + step)
    arrivals = [row_halos.at[0], row_halos.at[1], column_halos.at[0], column_halos.at[1]]
    arrivals += [corner_halos.at[end, side] for end in range(2) for side in range(2)]
    for slot, buffer in enumerate(arrivals):
        pltpu.make_async_remote_copy(
            src_ref=buffer, dst_ref=buffer, send_sem=send_halo.at[slot], recv_sem=recv_halo.at[slot],
            device_id=(band, sector), device_id_type=mesh_id).wait_recv()

    for end, lines in enumerate(((-1, -2), (TILE_ROWS, TILE_ROWS + 1))):
        for depth, line in enumerate(lines):
            field[pl.ds(at(line, 0), TILE_COLS), :] = row_halos[end, depth].astype(f32)
    for side, columns in enumerate(((-1, -2), (TILE_COLS, TILE_COLS + 1))):
        for depth, column in enumerate(columns):
            for line in range(TILE_ROWS):
                field[pl.ds(at(line, column), 1), :] = column_halos[side, depth, pl.ds(line, 1), :]
        for end, lines in enumerate(((-1, -2), (TILE_ROWS, TILE_ROWS + 1))):
            for i, line in enumerate(lines):
                for j, column in enumerate(columns):
                    field[pl.ds(at(line, column), 1), :] = corner_halos[end, side, pl.ds(2 * i + j, 1), :]

    def spread(array, start, stop):
        for tap in range(3):
            shifted[pl.ds(start, stop - start), tap * width:(tap + 1) * width] = (
                array[pl.ds(start + tap - 1, stop - start), :].astype(bf16))

    low, high = at(-1, -16), at(TILE_ROWS, PITCH)
    spread(field, low - PITCH, high + PITCH)
    total = 0.0
    for tap in range(3):
        total += jnp.dot(shifted[pl.ds(low + (tap - 1) * PITCH, high - low), :], first_kernel[tap],
                         preferred_element_type=f32)
    tall = PITCH + 16
    turned = 0.0
    for tap in range(3):
        lines = jnp.concatenate(
            [shifted[pl.ds(at(line - (tap - 1), -16), tall), :] for line in (-1, TILE_ROWS)], axis=0)
        turned += jnp.dot(lines, first_kernel[tap], preferred_element_type=f32)
    half_bias = 0.5 * bias_ref[...]

    def activate(value):
        half = 0.5 * value + half_bias
        return half + half * jnp.tanh(half)

    middle[pl.ds(low, high - low), :] = activate(total)
    turned = activate(turned)
    spot = lax.broadcasted_iota(i32, (tall, width), 0)
    inside = (spot >= 15) & (spot < 16 + TILE_COLS + 1)
    for index, (line, polar) in enumerate(((-1, band == 0), (TILE_ROWS, band == bands - 1))):
        place = pl.ds(at(line, -16), tall)
        chosen = jnp.where(polar, 1, 0)
        middle[place, :] = jnp.where(
            inside & (chosen == 1), turned[index * tall:(index + 1) * tall], middle[place, :])

    start, stop = at(0, 0), at(TILE_ROWS, 0)
    spread(middle, start - PITCH, stop + PITCH)
    total = field[pl.ds(start, stop - start), :]
    for tap in range(3):
        total += jnp.dot(shifted[pl.ds(start + (tap - 1) * PITCH, stop - start), :], second_kernel[tap],
                         preferred_element_type=f32)
    out_ref[...] = total.reshape(TILE_ROWS, PITCH, width)[:, :TILE_COLS].astype(bf16)
    for copy in copies:
        copy.wait_send()


def partner(step):
    core = lax.rem(step, 2)
    along = lax.rem(lax.div(step, 2), 4)
    half = lax.rem(lax.div(step, 8), 2)
    turn = lax.rem(lax.div(step, 16), 4)
    last = lax.div(step, 64)
    sector = lax.axis_index("lon")
    own_x, own_y, own_core = lax.div(sector, 8), lax.rem(lax.div(sector, 2), 4), lax.rem(sector, 2)
    to_x = lax.rem(own_x + along, 4)
    to_y = lax.rem(own_y + along + turn, 4)
    to_core = lax.rem(own_core + core, 2)
    to_band = lax.rem(lax.axis_index("lat") + along + 2 * half + last, 4)
    return to_band, to_x * 8 + to_y * 2 + to_core


def order_rows(shards, capacity, dest, cell, obs, waits, greet, source, ordered, spots, table, order, order_smem,
               begins, begins_smem, copy_sem):
    values, count_rows = obs.shape
    packing = 128 // values
    f32, bf16, i32 = jnp.float32, jnp.bfloat16, jnp.int32
    lines = count_rows // 128
    span = 4 * BLOCK

    band, sector = partner(lax.broadcasted_iota(i32, (shards, 1), 0))
    owner = band * lax.axis_size("lon") + sector
    lane = lax.broadcasted_iota(i32, (BLOCK, BLOCK + 128), 1)
    row = lax.broadcasted_iota(i32, (BLOCK, BLOCK + 128), 0)
    earlier = jnp.where((row < lane) | (lane >= BLOCK), 1.0, 0.0).astype(bf16)
    value_lane = lax.broadcasted_iota(i32, (values, 128), 1)
    value_row = lax.broadcasted_iota(i32, (values, 128), 0)
    spread = jnp.where(lax.rem(value_lane, values) == value_row, 1.0, 0.0).astype(bf16)
    ranks = lax.broadcasted_iota(i32, (capacity, BLOCK), 0).astype(f32)
    high_lines = lax.broadcasted_iota(i32, (lines, BLOCK), 0)
    low_lines = lax.broadcasted_iota(i32, (128, BLOCK), 0)
    number_lane = lax.broadcasted_iota(i32, (1, BLOCK), 1).astype(f32)

    table[...] = jnp.zeros_like(table)
    order[...] = jnp.zeros_like(order)
    ordered[pl.ds(count_rows, capacity), :] = jnp.zeros((capacity, 128), f32)
    waits[0].wait()

    def count(step, total):
        at = pl.multiple_of(step * (count_rows // 32), count_rows // 32)
        for part in range(count_rows // 32 // 128):
            total += jnp.where(owner == dest[:, pl.ds(at + 128 * part, 128)], 1.0, 0.0)
        for part in range(shards // 32):
            greet(step * (shards // 32) + part)
        return total

    total = lax.fori_loop(0, 32, count, jnp.zeros((shards, 128), f32))
    below = lax.broadcasted_iota(i32, (shards, shards), 0) > lax.broadcasted_iota(i32, (shards, shards), 1)
    begin = jnp.dot(jnp.where(below, 1.0, 0.0).astype(bf16), total.astype(bf16), preferred_element_type=f32)
    begin = jnp.sum(begin, axis=1, keepdims=True)
    begins[...] = jnp.broadcast_to(jnp.clip(begin.astype(i32), 0, count_rows), begins.shape)
    begins_copy = pltpu.make_async_copy(begins, begins_smem, copy_sem.at[0])
    begins_copy.start()
    waits[1].wait()
    waits[2].wait()

    def place(step, carry):
        weights, ranked, highs, lows = [], [], [], []
        for part in range(span // BLOCK):
            at = pl.multiple_of(step * span + part * BLOCK, BLOCK)
            named = jnp.where(owner == dest[:, pl.ds(at, BLOCK)], 1.0, 0.0)
            counted = jnp.dot(named.astype(bf16), earlier, preferred_element_type=f32)
            before = counted[:, :BLOCK] + jnp.concatenate([carry] * (BLOCK // 128), axis=1)
            carry = carry + counted[:, BLOCK:]
            rank = jnp.sum(named * before, axis=0, keepdims=True)
            spot = (rank + jnp.sum(named * begin, axis=0, keepdims=True)).astype(i32)
            cells = cell[:, pl.ds(at, BLOCK)]
            high = lax.shift_right_logical(cells, 6)
            low = cells - lax.shift_left(high, 6)
            weights.append(jnp.concatenate(
                [named * (high + 1).astype(f32), named * low.astype(f32)], axis=0).astype(bf16))
            ranked.append(jnp.where(ranks == rank, 1.0, 0.0).astype(bf16))
            spot_high = lax.shift_right_logical(spot, 7)
            spot_low = spot - lax.shift_left(spot_high, 7)
            here = high_lines == spot_high
            block_number = (step * (span // BLOCK) + part).astype(f32)
            highs.append(jnp.concatenate(
                [jnp.where(here, block_number, 0.0), jnp.where(here, number_lane, 0.0)], axis=0).astype(bf16))
            lows.append(jnp.where(low_lines == spot_low, 1.0, 0.0).astype(bf16))
            source[pl.ds(at, BLOCK), :] = lax.dot_general(
                obs[:, pl.ds(at, BLOCK)].astype(bf16), spread, (((0,), (0,)), ((), ())), preferred_element_type=f32)
        along = (((1,), (1,)), ((), ()))
        table[...] += lax.dot_general(
            jnp.concatenate(weights, axis=1), jnp.concatenate(ranked, axis=1), along, preferred_element_type=f32)
        order[...] += lax.dot_general(
            jnp.concatenate(highs, axis=1), jnp.concatenate(lows, axis=1), along, preferred_element_type=f32)
        return carry

    lax.fori_loop(0, count_rows // span, place, jnp.zeros((shards, 128), f32))

    numbers = order[:lines, :].astype(i32) * BLOCK + order[lines:, :].astype(i32)
    begins_copy.wait()
    begins[pl.ds(0, lines), :] = jnp.clip(numbers, 0, count_rows - 1)
    order_copy = pltpu.make_async_copy(begins.at[pl.ds(0, lines)], order_smem, copy_sem.at[1])
    order_copy.start()
    found = table[:shards, :].astype(i32) * 64 + table[shards:, :].astype(i32) - 64
    found = jnp.where(found >= 0, found, -1)
    absent = jnp.full((shards, 64), -1, i32)
    straight = jnp.concatenate([found, absent], axis=1)
    turned = jnp.concatenate([absent, found], axis=1)
    odd = lax.rem(lax.broadcasted_iota(i32, (shards, 1), 0), 2)
    placed = jnp.where(odd == 1, turned, straight)
    spots[:, 0, :] = placed[:, :128]
    spots[:, 1, :] = placed[:, 128:]
    order_copy.wait()


def exchange_kernel(group, chunk, obs_ref, dest_ref, cell_ref, first_ref, bias_ref, second_ref,
                    conv_first_ref, conv_bias_ref, conv_second_ref, out_ref,
                    obs, dest, cell, source, ordered, table, order, order_smem, begins, begins_smem,
                    outbox, spots, rows_got, cells_got, features, sums, counts, first_kernel, second_kernel,
                    field, shifted, middle,
                    row_edges, column_edges, corner_edges, row_halos, column_halos, corner_halos, own_sem, copy_sem,
                    send_rows, send_cells, recv_rows, recv_cells, send_halo, recv_halo):
    shards, packed, _ = rows_got.shape
    values = first_ref.shape[0]
    width = second_ref.shape[1]
    packing = 128 // values
    capacity = packing * packed
    count_rows = obs.shape[1]
    tile_cells = TILE_ROWS * TILE_COLS
    f32, bf16, i32 = jnp.float32, jnp.bfloat16, jnp.int32
    mesh_id = pl.DeviceIdType.MESH

    barrier = pltpu.get_barrier_semaphore()
    loads = [
        pltpu.make_async_copy(source_ref, target, own_sem.at[number])
        for number, (source_ref, target) in enumerate((
            (dest_ref, dest), (cell_ref, cell), (obs_ref, obs), (conv_first_ref, first_kernel),
            (conv_second_ref, second_kernel)))
    ]
    for copy in loads:
        copy.start()
    kernels = loads[3:]

    def greet(step):
        @pl.when(step > 0)
        def _():
            pl.semaphore_signal(barrier, inc=1, device_id=partner(step), device_id_type=mesh_id)

    order_rows(shards, capacity, dest, cell, obs, loads[:3], greet, source, ordered, spots, table, order, order_smem,
               begins, begins_smem, copy_sem)
    pl.semaphore_wait(barrier, shards - 1)

    def copies(step):
        target = partner(step)
        return (
            pltpu.make_async_remote_copy(
                src_ref=outbox.at[step], dst_ref=rows_got.at[step], send_sem=send_rows.at[step],
                recv_sem=recv_rows.at[step], device_id=target, device_id_type=mesh_id),
            pltpu.make_async_remote_copy(
                src_ref=spots.at[step], dst_ref=cells_got.at[step], send_sem=send_cells.at[step],
                recv_sem=recv_cells.at[step], device_id=target, device_id_type=mesh_id),
        )

    plane_of = lax.broadcasted_iota(i32, (packed, 128), 1) // values

    def pack(step):
        begin = begins_smem[step, 0] & (ROOM - 1)
        rows = ordered[pl.ds(begin, packed), :]
        for plane in range(1, packing):
            rows = jnp.where(plane_of == plane, ordered[pl.ds(begin + plane * packed, packed), :], rows)
        return rows.astype(bf16)

    def send(step):
        outbox[step] = pack(step)
        for copy in copies(step):
            copy.start()

    pair = 2 * capacity

    def gather(turn, _):
        at = pl.multiple_of(turn * pair, pair)
        for line in range(pair // 128):
            for lane in range(128):
                number = order_smem[turn * (pair // 128) + line, lane] & (ROOM - 1)
                ordered[pl.ds(at + line * 128 + lane, 1), :] = source[pl.ds(number, 1), :]

        @pl.when(turn == 0)
        def _():
            rows_got[0] = pack(0)
            cells_got[0] = spots[0]

        @pl.when(turn > 0)
        def _():
            send(2 * turn)

        send(2 * turn + 1)
        return 0

    lax.fori_loop(0, count_rows // pair, gather, 0)

    def send_rest(step, _):
        send(step)
        return 0

    lax.fori_loop(2 * (count_rows // pair), shards, send_rest, 0)

    sums[...] = jnp.zeros_like(sums)
    counts[...] = jnp.zeros_like(counts)
    first = first_ref[...]
    first_high = first.astype(bf16)
    first_low = (first - first_high.astype(f32)).astype(bf16)
    blank = jnp.zeros((values, width), bf16)
    weights = []
    for plane in range(packing):
        pieces = [blank] * (2 * packing)
        pieces[plane] = first_high
        pieces[packing + plane] = first_low
        weights.append(jnp.concatenate(pieces, axis=0))
    half_bias = 0.5 * bias_ref[...]
    lane = lax.broadcasted_iota(i32, (1, 128), 1)

    def receive(step, _):
        for copy in copies(step):
            copy.wait_recv()
        return 0

    def work(number, _):
        base = number * group
        lax.fori_loop(jnp.maximum(base, 1), base + group, receive, 0)
        rows = rows_got[pl.ds(base, group)].reshape(group * packed, 128)
        rows = jnp.concatenate([rows, rows], axis=1)
        for plane in range(packing):
            half = 0.5 * jnp.dot(rows, weights[plane], preferred_element_type=f32) + half_bias
            hidden = (half + half * jnp.tanh(half)).astype(bf16)
            made = jnp.dot(hidden, second_ref[...], preferred_element_type=f32).astype(bf16)
            features[:, plane] = made.reshape(group, packed, width)
        for part in range(group // chunk):
            pieces = []
            for pair in range(part * chunk // 2, (part + 1) * chunk // 2):
                even = cells_got[base + 2 * pair]
                odd = cells_got[base + 2 * pair + 1]
                pieces += [even[0:1], jnp.where(lane < 64, even[1:2], odd[0:1]), odd[1:2]]
            cell = jnp.concatenate(pieces, axis=1)
            span = chunk * capacity
            spots = lax.broadcasted_iota(jnp.int16, (tile_cells, span), 0)
            onehot = jnp.where(spots == cell.astype(jnp.int16), 1.0, 0.0).astype(bf16)
            sums[...] += jnp.dot(
                onehot, features[pl.ds(part * chunk, chunk)].reshape(span, width), preferred_element_type=f32)
            line = lax.shift_right_arithmetic(cell * 1366, 16)
            column = cell - line * TILE_COLS
            lines = jnp.where(lax.broadcasted_iota(i32, (32, span), 0) == line, 1.0, 0.0).astype(bf16)
            columns = jnp.where(
                (lax.broadcasted_iota(i32, (TILE_COLS, span), 0) == column) & (cell >= 0), 1.0, 0.0).astype(bf16)
            counts[...] += lax.dot_general(columns, lines, (((1,), (1,)), ((), ())), preferred_element_type=f32)
        return 0

    lax.fori_loop(0, shards // group, work, 0)

    scale = 1.0 / jnp.maximum(counts[...], 1.0)
    for copy in kernels:
        copy.wait()
    encode_tile(sums, scale, first_kernel, second_kernel, conv_bias_ref, out_ref, field, shifted, middle,
                row_edges, column_edges, corner_edges, row_halos, column_halos, corner_halos, send_halo, recv_halo)

    def drain(step, _):
        for copy in copies(step):
            copy.wait_send()
        return 0

    lax.fori_loop(1, shards, drain, 0)


def exchange(observations, destinations, cells, first_weight, first_bias, second_weight, conv_first, conv_bias,
             conv_second, shards, capacity, group=16, chunk=4):
    count_rows, values = observations.shape
    width = second_weight.shape[1]
    vmem = pl.BlockSpec(memory_space=pltpu.VMEM)
    anywhere = pl.BlockSpec(memory_space=pl.ANY)
    packing = 128 // values
    packed = capacity // packing
    lines = count_rows // 128
    field_rows = (TILE_ROWS + 5) * PITCH + 16
    dma = pltpu.SemaphoreType.DMA
    f32, bf16, i32 = jnp.float32, jnp.bfloat16, jnp.int32
    return pl.pallas_call(
        functools.partial(exchange_kernel, group, chunk),
        out_shape=jax.ShapeDtypeStruct((TILE_ROWS, TILE_COLS, width), bf16),
        in_specs=[anywhere, anywhere, anywhere, vmem, vmem, vmem, anywhere, vmem, anywhere],
        out_specs=vmem,
        scratch_shapes=[
            pltpu.VMEM((values, count_rows), f32),
            pltpu.VMEM((1, count_rows), i32),
            pltpu.VMEM((1, count_rows), i32),
            pltpu.VMEM((ROOM, 128), f32),
            pltpu.VMEM((ROOM + capacity, 128), f32),
            pltpu.VMEM((2 * shards, capacity), f32),
            pltpu.VMEM((2 * lines, 128), f32),
            pltpu.SMEM((lines, 128), i32),
            pltpu.VMEM((shards, 128), i32),
            pltpu.SMEM((shards, 128), i32),
            pltpu.VMEM((shards, packed, 128), bf16),
            pltpu.VMEM((shards, 2, 128), i32),
            pltpu.VMEM((shards, packed, 128), bf16),
            pltpu.VMEM((shards, 2, 128), i32),
            pltpu.VMEM((group, packing, packed, width), bf16),
            pltpu.VMEM((TILE_ROWS * TILE_COLS, width), f32),
            pltpu.VMEM((TILE_COLS, 32), f32),
            pltpu.VMEM((3, 3 * width, width), bf16),
            pltpu.VMEM((3, 3 * width, width), bf16),
            pltpu.VMEM((field_rows, width), f32),
            pltpu.VMEM((field_rows, 3 * width), bf16),
            pltpu.VMEM((field_rows, width), f32),
            pltpu.VMEM((2, 2, TILE_COLS, width), bf16),
            pltpu.VMEM((2, 2, TILE_ROWS, width), f32),
            pltpu.VMEM((2, 2, 8, width), f32),
            pltpu.VMEM((2, 2, TILE_COLS, width), bf16),
            pltpu.VMEM((2, 2, TILE_ROWS, width), f32),
            pltpu.VMEM((2, 2, 8, width), f32),
            dma((5,)), dma((2,)), dma((shards,)), dma((shards,)), dma((shards,)), dma((shards,)),
            dma((8,)), dma((8,)),
        ],
        compiler_params=pltpu.CompilerParams(
            collective_id=0, has_side_effects=True, vmem_limit_bytes=56 * 1024 * 1024),
        name="exchange",
    )(observations.T, destinations.reshape(1, -1), cells.reshape(1, -1), first_weight, first_bias.reshape(1, -1),
      second_weight, conv_first.reshape(3, 3 * width, width), conv_bias.reshape(1, -1),
      conv_second.reshape(3, 3 * width, width))


def body(
    observations,
    destinations,
    cells,
    first_weight,
    first_bias,
    second_weight,
    conv_first,
    conv_bias,
    conv_second,
):
    shards = lax.axis_size("lat") * lax.axis_size("lon")
    capacity = 2 * observations.shape[0] // shards
    return exchange(observations, destinations, cells, first_weight, first_bias, second_weight, conv_first, conv_bias,
                    conv_second, shards, capacity)


def solution(mesh):
    in_specs = (
        P(("lat", "lon"), None),
        P(("lat", "lon"), None),
        P(("lat", "lon")),
        P(),
        P(),
        P(),
        P(),
        P(),
        P(),
    )
    out_specs = P("lat", "lon", None)
    return jax.shard_map(body, mesh=mesh, in_specs=in_specs, out_specs=out_specs, check_vma=False)
```

time: 101 us -> 88.5 us (0.88)
  Pallas kernels: 95.3 us -> 86.2 us
  local copies, waits for them, and re-layouts: 5.13 us -> 1.92 us
    pallas_call x2 -> x1, Pallas kernels: 95.3 us -> 86.2 us  [exchange(): pl.pallas_call(functools.partial(exchange_kernel, group, chunk), out_shap...]
    unnamed x19 -> x1, local copies, waits for them, and re-layouts: 5.13 us -> 1.92 us
where the time goes in v2:
time: 88.5 us; the launch traced here: 88.1 us
  Pallas kernels  86.2 us (97%)
  local copies, waits for them, and re-layouts  1.92 us (2%)
    pallas_call x1, Pallas kernels, exchange(): pl.pallas_call(functools.partial(exchange_kernel, group, chunk), out_shap...  86.2 us
    unnamed x1, local copies, waits for them, and re-layouts  1.92 us

profile of v2, /device:TPU:0, one launch (start us, length us, event | category | flops | bytes accessed | tf_op | source)
XLA Modules:
  0.0 88.1 jit_solution(7360144663738474315)
XLA Ops:
  0.0 86.2 %exchange.1 = bf16[24,48,256]{2,1,0:T(8,128)(2,1)} custom-call(f32[32,12288]{1,0:T(8,128)} %bitcast.7, s32[1,12288]{1,0:T(1,128)} %bitcast.10, s32[1,12288]{1,0:T(1,128)} %bitcast.11, f32[32,256]{1,0:T(8,128)} %first_ref.1, f32[1,256]{1,0:T(1,128)} %bitcast.12, bf16[256,256]{1,0:T(8,128)(2,1)} %second_ref.1, bf16[3,768,256]{2,1,0:T(8,128)(2,1)} %bitcast.8, ...), custom_call_target="tpu_custom_call" | custom-call | tf_op jit(solution)/shard_map/exchange/pallas_call | solution.py:413
  86.2 1.9 %copy.11 = bf16[24,48,256]{2,1,0:T(8,128)(2,1)} copy(bf16[24,48,256]{2,1,0:T(8,128)(2,1)} %exchange.1) | data formatting | bytes 1179648

commit v3 on v2

--- a/solution.py
+++ b/solution.py
@@ -309,7 +309,7 @@
         at = pl.multiple_of(turn * pair, pair)
         for line in range(pair // 128):
             for lane in range(128):
-                number = order_smem[turn * (pair // 128) + line, lane] & (ROOM - 1)
+                number = order_smem[turn * (pair // 128) + line, lane]
                 ordered[pl.ds(at + line * 128 + lane, 1), :] = source[pl.ds(number, 1), :]
 
         @pl.when(turn == 0)
@@ -370,8 +370,8 @@
                 pieces += [even[0:1], jnp.where(lane < 64, even[1:2], odd[0:1]), odd[1:2]]
             cell = jnp.concatenate(pieces, axis=1)
             span = chunk * capacity
-            spots = lax.broadcasted_iota(jnp.int16, (tile_cells, span), 0)
-            onehot = jnp.where(spots == cell.astype(jnp.int16), 1.0, 0.0).astype(bf16)
+            spots = lax.broadcasted_iota(i32, (tile_cells, span), 0)
+            onehot = jnp.where(spots == cell, 1.0, 0.0).astype(bf16)
             sums[...] += jnp.dot(
                 onehot, features[pl.ds(part * chunk, chunk)].reshape(span, width), preferred_element_type=f32)
             line = lax.shift_right_arithmetic(cell * 1366, 16)

time: 88.5 us -> 81.9 us (0.925)
  Pallas kernels: 86.2 us -> 79.6 us
    pallas_call x1, Pallas kernels: 86.2 us -> 79.6 us  [exchange(): pl.pallas_call(functools.partial(exchange_kernel, group, chunk), out_shap...]
where the time goes in v3:
time: 81.9 us; the launch traced here: 81.6 us
  Pallas kernels  79.6 us (97%)
  local copies, waits for them, and re-layouts  1.92 us (2%)
    pallas_call x1, Pallas kernels, exchange(): pl.pallas_call(functools.partial(exchange_kernel, group, chunk), out_shap...  79.6 us
    unnamed x1, local copies, waits for them, and re-layouts  1.92 us

profile of v3, /device:TPU:0, one launch (start us, length us, event | category | flops | bytes accessed | tf_op | source)
XLA Modules:
  0.0 81.6 jit_solution(15862915606497323717)
XLA Ops:
  0.0 79.6 %exchange.1 = bf16[24,48,256]{2,1,0:T(8,128)(2,1)} custom-call(f32[32,12288]{1,0:T(8,128)} %bitcast.7, s32[1,12288]{1,0:T(1,128)} %bitcast.10, s32[1,12288]{1,0:T(1,128)} %bitcast.11, f32[32,256]{1,0:T(8,128)} %first_ref.1, f32[1,256]{1,0:T(1,128)} %bitcast.12, bf16[256,256]{1,0:T(8,128)(2,1)} %second_ref.1, bf16[3,768,256]{2,1,0:T(8,128)(2,1)} %bitcast.8, ...), custom_call_target="tpu_custom_call" | custom-call | tf_op jit(solution)/shard_map/exchange/pallas_call | solution.py:413
  79.6 1.9 %copy.11 = bf16[24,48,256]{2,1,0:T(8,128)(2,1)} copy(bf16[24,48,256]{2,1,0:T(8,128)(2,1)} %exchange.1) | data formatting | bytes 1179648

commit v4 on v3

--- a/solution.py
+++ b/solution.py
@@ -17,7 +17,7 @@
 
 
 def encode_tile(sums, scale, first_kernel, second_kernel, bias_ref, out_ref, field, shifted, middle,
-                row_edges, column_edges, corner_edges, row_halos, column_halos, corner_halos,
+                column_stage, row_edges, column_edges, corner_edges, row_halos, column_halos, corner_halos,
                 send_halo, recv_halo):
     f32, bf16, i32 = jnp.float32, jnp.bfloat16, jnp.int32
     mesh_id = pl.DeviceIdType.MESH
@@ -27,23 +27,6 @@
 
     def at(line, column):
         return (line + 3) * PITCH + column
-
-    for line in range(TILE_ROWS):
-        block = sums[pl.ds(line * TILE_COLS, TILE_COLS), :] * scale[:, line:line + 1]
-        block = block.astype(bf16)
-        field[pl.ds(at(line, 0), TILE_COLS), :] = block.astype(f32)
-        if line < 2:
-            row_edges[0, line] = block
-        if line >= TILE_ROWS - 2:
-            row_edges[1, TILE_ROWS - 1 - line] = block
-    for side, columns in enumerate(((0, 1), (TILE_COLS - 1, TILE_COLS - 2))):
-        for depth, column in enumerate(columns):
-            for line in range(TILE_ROWS):
-                column_edges[side, depth, pl.ds(line, 1), :] = field[pl.ds(at(line, column), 1), :]
-        for end, lines in enumerate(((0, 1), (TILE_ROWS - 1, TILE_ROWS - 2))):
-            for i, line in enumerate(lines):
-                for j, column in enumerate(columns):
-                    corner_edges[end, side, pl.ds(2 * i + j, 1), :] = field[pl.ds(at(line, column), 1), :]
 
     north = band > 0
     south = band < bands - 1
@@ -60,14 +43,34 @@
                 device_id=(target_band, lax.rem(sector + shift + 2 * sectors, sectors)), device_id_type=mesh_id))
         copies[-1].start()
 
+    def average(line):
+        block = sums[pl.ds(line * TILE_COLS, TILE_COLS), :] * scale[:, line:line + 1]
+        block = block.astype(bf16)
+        field[pl.ds(at(line, 0), TILE_COLS), :] = block.astype(f32)
+        return block
+
+    ends = ((0, 1), (TILE_ROWS - 1, TILE_ROWS - 2))
+    borders = ((0, 1), (TILE_COLS - 1, TILE_COLS - 2))
     for end, (target_band, shift, landing) in enumerate(vertical):
+        for depth, line in enumerate(ends[end]):
+            row_edges[end, depth] = average(line)
         ship(row_edges.at[end], row_halos.at[landing], landing, target_band, shift)
-    for side, step in enumerate((-1, 1)):
-        ship(column_edges.at[side], column_halos.at[1 - side], 2 + 1 - side, band, step)
     for end, (target_band, shift, landing) in enumerate(vertical):
         for side, step in enumerate((-1, 1)):
+            for i, line in enumerate(ends[end]):
+                for j, column in enumerate(borders[side]):
+                    corner_edges[end, side, pl.ds(2 * i + j, 1), :] = field[pl.ds(at(line, column), 1), :]
             ship(corner_edges.at[end, side], corner_halos.at[landing, 1 - side], 4 + 2 * landing + 1 - side,
                  target_band, shift + step)
+    for line in range(2, TILE_ROWS - 2):
+        average(line)
+    blank = jnp.zeros((8, width), f32)
+    for side, step in enumerate((-1, 1)):
+        for depth, column in enumerate(borders[side]):
+            for line in range(TILE_ROWS):
+                column_stage[side, depth, pl.ds(line, 1), :] = field[pl.ds(at(line, column), 1), :]
+            column_edges[side, depth] = jnp.concatenate([column_stage[side, depth], blank], axis=0).astype(bf16)
+        ship(column_edges.at[side], column_halos.at[1 - side], 2 + 1 - side, band, step)
     arrivals = [row_halos.at[0], row_halos.at[1], column_halos.at[0], column_halos.at[1]]
     arrivals += [corner_halos.at[end, side] for end in range(2) for side in range(2)]
     for slot, buffer in enumerate(arrivals):
@@ -80,8 +83,9 @@
             field[pl.ds(at(line, 0), TILE_COLS), :] = row_halos[end, depth].astype(f32)
     for side, columns in enumerate(((-1, -2), (TILE_COLS, TILE_COLS + 1))):
         for depth, column in enumerate(columns):
+            column_stage[side, depth] = column_halos[side, depth].astype(f32)[:TILE_ROWS]
             for line in range(TILE_ROWS):
-                field[pl.ds(at(line, column), 1), :] = column_halos[side, depth, pl.ds(line, 1), :]
+                field[pl.ds(at(line, column), 1), :] = column_stage[side, depth, pl.ds(line, 1), :]
         for end, lines in enumerate(((-1, -2), (TILE_ROWS, TILE_ROWS + 1))):
             for i, line in enumerate(lines):
                 for j, column in enumerate(columns):
@@ -94,10 +98,9 @@
 
     low, high = at(-1, -16), at(TILE_ROWS, PITCH)
     spread(field, low - PITCH, high + PITCH)
-    total = 0.0
-    for tap in range(3):
-        total += jnp.dot(shifted[pl.ds(low + (tap - 1) * PITCH, high - low), :], first_kernel[tap],
-                         preferred_element_type=f32)
+    parts = [shifted[pl.ds(low + (tap - 1) * PITCH, high - low), :] for tap in range(3)]
+    total = jnp.dot(jnp.concatenate(parts, axis=1), first_kernel[...].reshape(9 * width, width),
+                    preferred_element_type=f32)
     tall = PITCH + 16
     turned = 0.0
     for tap in range(3):
@@ -123,9 +126,9 @@
     start, stop = at(0, 0), at(TILE_ROWS, 0)
     spread(middle, start - PITCH, stop + PITCH)
     total = field[pl.ds(start, stop - start), :]
-    for tap in range(3):
-        total += jnp.dot(shifted[pl.ds(start + (tap - 1) * PITCH, stop - start), :], second_kernel[tap],
-                         preferred_element_type=f32)
+    parts = [shifted[pl.ds(start + (tap - 1) * PITCH, stop - start), :] for tap in range(3)]
+    total += jnp.dot(jnp.concatenate(parts, axis=1), second_kernel[...].reshape(9 * width, width),
+                     preferred_element_type=f32)
     out_ref[...] = total.reshape(TILE_ROWS, PITCH, width)[:, :TILE_COLS].astype(bf16)
     for copy in copies:
         copy.wait_send()
@@ -146,7 +149,7 @@
     return to_band, to_x * 8 + to_y * 2 + to_core
 
 
-def order_rows(shards, capacity, dest, cell, obs, waits, greet, source, ordered, spots, table, order, order_smem,
+def order_rows(shards, capacity, dest, cell, obs, waits, source, ordered, spots, table, order, order_smem,
                begins, begins_smem, copy_sem):
     values, count_rows = obs.shape
     packing = 128 // values
@@ -176,8 +179,6 @@
         at = pl.multiple_of(step * (count_rows // 32), count_rows // 32)
         for part in range(count_rows // 32 // 128):
             total += jnp.where(owner == dest[:, pl.ds(at + 128 * part, 128)], 1.0, 0.0)
-        for part in range(shards // 32):
-            greet(step * (shards // 32) + part)
         return total
 
     total = lax.fori_loop(0, 32, count, jnp.zeros((shards, 128), f32))
@@ -222,7 +223,7 @@
             jnp.concatenate(highs, axis=1), jnp.concatenate(lows, axis=1), along, preferred_element_type=f32)
         return carry
 
-    lax.fori_loop(0, count_rows // span, place, jnp.zeros((shards, 128), f32))
+    lax.fori_loop(0, count_rows // span, place, jnp.zeros((shards, 128), f32), unroll=2)
 
     numbers = order[:lines, :].astype(i32) * BLOCK + order[lines:, :].astype(i32)
     begins_copy.wait()
@@ -246,7 +247,7 @@
                     obs, dest, cell, source, ordered, table, order, order_smem, begins, begins_smem,
                     outbox, spots, rows_got, cells_got, features, sums, counts, first_kernel, second_kernel,
                     field, shifted, middle,
-                    row_edges, column_edges, corner_edges, row_halos, column_halos, corner_halos, own_sem, copy_sem,
+                    column_stage, row_edges, column_edges, corner_edges, row_halos, column_halos, corner_halos, own_sem, copy_sem,
                     send_rows, send_cells, recv_rows, recv_cells, send_halo, recv_halo):
     shards, packed, _ = rows_got.shape
     values = first_ref.shape[0]
@@ -269,12 +270,21 @@
         copy.start()
     kernels = loads[3:]
 
-    def greet(step):
-        @pl.when(step > 0)
-        def _():
-            pl.semaphore_signal(barrier, inc=1, device_id=partner(step), device_id_type=mesh_id)
-
-    order_rows(shards, capacity, dest, cell, obs, loads[:3], greet, source, ordered, spots, table, order, order_smem,
+    band, sector = lax.axis_index("lat"), lax.axis_index("lon")
+    bands = [lax.rem(band + shift, 4) for shift in range(4)]
+    along_x = [8 * lax.rem(lax.div(sector, 8) + shift, 4) for shift in range(4)]
+    along_y = [2 * lax.rem(lax.div(sector, 2) + shift, 4) for shift in range(4)]
+    cores = [lax.rem(sector, 2), 1 - lax.rem(sector, 2)]
+    for x in along_x:
+        for y in along_y:
+            for core in cores:
+                place = x + y + core
+                for to_band in bands:
+                    if x is along_x[0] and y is along_y[0] and core is cores[0] and to_band is bands[0]:
+                        continue
+                    pl.semaphore_signal(barrier, inc=1, device_id=(to_band, place), device_id_type=mesh_id)
+
+    order_rows(shards, capacity, dest, cell, obs, loads[:3], source, ordered, spots, table, order, order_smem,
                begins, begins_smem, copy_sem)
     pl.semaphore_wait(barrier, shards - 1)
 
@@ -388,7 +398,7 @@
     for copy in kernels:
         copy.wait()
     encode_tile(sums, scale, first_kernel, second_kernel, conv_bias_ref, out_ref, field, shifted, middle,
-                row_edges, column_edges, corner_edges, row_halos, column_halos, corner_halos, send_halo, recv_halo)
+                column_stage, row_edges, column_edges, corner_edges, row_halos, column_halos, corner_halos, send_halo, recv_halo)
 
     def drain(step, _):
         for copy in copies(step):
@@ -438,12 +448,13 @@
             pltpu.VMEM((field_rows, width), f32),
             pltpu.VMEM((field_rows, 3 * width), bf16),
             pltpu.VMEM((field_rows, width), f32),
+            pltpu.VMEM((2, 2, TILE_ROWS, width), f32),
             pltpu.VMEM((2, 2, TILE_COLS, width), bf16),
-            pltpu.VMEM((2, 2, TILE_ROWS, width), f32),
-            pltpu.VMEM((2, 2, 8, width), f32),
+            pltpu.VMEM((2, 2, 32, width), bf16),
+            pltpu.VMEM((2, 2, 4, width), f32),
             pltpu.VMEM((2, 2, TILE_COLS, width), bf16),
-            pltpu.VMEM((2, 2, TILE_ROWS, width), f32),
-            pltpu.VMEM((2, 2, 8, width), f32),
+            pltpu.VMEM((2, 2, 32, width), bf16),
+            pltpu.VMEM((2, 2, 4, width), f32),
             dma((5,)), dma((2,)), dma((shards,)), dma((shards,)), dma((shards,)), dma((shards,)),
             dma((8,)), dma((8,)),
         ],

time: 81.9 us -> 76.7 us (0.937)
  Pallas kernels: 79.6 us -> 74.6 us
    pallas_call x1, Pallas kernels: 79.6 us -> 74.6 us  [exchange(): pl.pallas_call(functools.partial(exchange_kernel, group, chunk), out_shap...]
where the time goes in v4:
time: 76.7 us; the launch traced here: 76.5 us
  Pallas kernels  74.6 us (97%)
  local copies, waits for them, and re-layouts  1.92 us (3%)
    pallas_call x1, Pallas kernels, exchange(): pl.pallas_call(functools.partial(exchange_kernel, group, chunk), out_shap...  74.6 us
    unnamed x1, local copies, waits for them, and re-layouts  1.92 us

profile of v4, /device:TPU:0, one launch (start us, length us, event | category | flops | bytes accessed | tf_op | source)
XLA Modules:
  0.0 76.5 jit_solution(5177597357587346347)
XLA Ops:
  0.0 74.6 %exchange.1 = bf16[24,48,256]{2,1,0:T(8,128)(2,1)} custom-call(f32[32,12288]{1,0:T(8,128)} %bitcast.7, s32[1,12288]{1,0:T(1,128)} %bitcast.10, s32[1,12288]{1,0:T(1,128)} %bitcast.11, f32[32,256]{1,0:T(8,128)} %first_ref.1, f32[1,256]{1,0:T(1,128)} %bitcast.12, bf16[256,256]{1,0:T(8,128)(2,1)} %second_ref.1, bf16[3,768,256]{2,1,0:T(8,128)(2,1)} %bitcast.8, ...), custom_call_target="tpu_custom_call" | custom-call | tf_op jit(solution)/shard_map/exchange/pallas_call | solution.py:423
  74.6 1.9 %copy.11 = bf16[24,48,256]{2,1,0:T(8,128)(2,1)} copy(bf16[24,48,256]{2,1,0:T(8,128)(2,1)} %exchange.1) | data formatting | bytes 1179648

commit v5 on v4

--- a/solution.py
+++ b/solution.py
@@ -134,18 +134,22 @@
         copy.wait_send()
 
 
-def partner(step):
+def own_place():
+    sector = lax.axis_index("lon")
+    return lax.axis_index("lat"), lax.div(sector, 8), lax.rem(lax.div(sector, 2), 4), lax.rem(sector, 2)
+
+
+def partner(step, own):
+    own_band, own_x, own_y, own_core = own
     core = lax.rem(step, 2)
     along = lax.rem(lax.div(step, 2), 4)
     half = lax.rem(lax.div(step, 8), 2)
     turn = lax.rem(lax.div(step, 16), 4)
     last = lax.div(step, 64)
-    sector = lax.axis_index("lon")
-    own_x, own_y, own_core = lax.div(sector, 8), lax.rem(lax.div(sector, 2), 4), lax.rem(sector, 2)
     to_x = lax.rem(own_x + along, 4)
     to_y = lax.rem(own_y + along + turn, 4)
     to_core = lax.rem(own_core + core, 2)
-    to_band = lax.rem(lax.axis_index("lat") + along + 2 * half + last, 4)
+    to_band = lax.rem(own_band + along + 2 * half + last, 4)
     return to_band, to_x * 8 + to_y * 2 + to_core
 
 
@@ -157,7 +161,7 @@
     lines = count_rows // 128
     span = 4 * BLOCK
 
-    band, sector = partner(lax.broadcasted_iota(i32, (shards, 1), 0))
+    band, sector = partner(lax.broadcasted_iota(i32, (shards, 1), 0), own_place())
     owner = band * lax.axis_size("lon") + sector
     lane = lax.broadcasted_iota(i32, (BLOCK, BLOCK + 128), 1)
     row = lax.broadcasted_iota(i32, (BLOCK, BLOCK + 128), 0)
@@ -223,7 +227,7 @@
             jnp.concatenate(highs, axis=1), jnp.concatenate(lows, axis=1), along, preferred_element_type=f32)
         return carry
 
-    lax.fori_loop(0, count_rows // span, place, jnp.zeros((shards, 128), f32), unroll=2)
+    lax.fori_loop(0, count_rows // span, place, jnp.zeros((shards, 128), f32), unroll=12)
 
     numbers = order[:lines, :].astype(i32) * BLOCK + order[lines:, :].astype(i32)
     begins_copy.wait()
@@ -288,8 +292,10 @@
                begins, begins_smem, copy_sem)
     pl.semaphore_wait(barrier, shards - 1)
 
+    own = own_place()
+
     def copies(step):
-        target = partner(step)
+        target = partner(step, own)
         return (
             pltpu.make_async_remote_copy(
                 src_ref=outbox.at[step], dst_ref=rows_got.at[step], send_sem=send_rows.at[step],
@@ -336,11 +342,12 @@
 
     lax.fori_loop(0, count_rows // pair, gather, 0)
 
-    def send_rest(step, _):
-        send(step)
+    def send_rest(turn, _):
+        for part in range(4):
+            send(4 * turn + part)
         return 0
 
-    lax.fori_loop(2 * (count_rows // pair), shards, send_rest, 0)
+    lax.fori_loop(count_rows // pair // 2, shards // 4, send_rest, 0)
 
     sums[...] = jnp.zeros_like(sums)
     counts[...] = jnp.zeros_like(counts)

time: 76.7 us -> 75.1 us (0.979)
  Pallas kernels: 74.6 us -> 73 us
    pallas_call x1, Pallas kernels: 74.6 us -> 73 us  [exchange(): pl.pallas_call(functools.partial(exchange_kernel, group, chunk), out_shap...]
where the time goes in v5:
time: 75.1 us; the launch traced here: 74.9 us
  Pallas kernels  73 us (97%)
  local copies, waits for them, and re-layouts  1.92 us (3%)
    pallas_call x1, Pallas kernels, exchange(): pl.pallas_call(functools.partial(exchange_kernel, group, chunk), out_shap...  73 us
    unnamed x1, local copies, waits for them, and re-layouts  1.92 us

profile of v5, /device:TPU:0, one launch (start us, length us, event | category | flops | bytes accessed | tf_op | source)
XLA Modules:
  0.0 74.9 jit_solution(10892680328004882821)
XLA Ops:
  0.0 73.0 %exchange.1 = bf16[24,48,256]{2,1,0:T(8,128)(2,1)} custom-call(f32[32,12288]{1,0:T(8,128)} %bitcast.7, s32[1,12288]{1,0:T(1,128)} %bitcast.10, s32[1,12288]{1,0:T(1,128)} %bitcast.11, f32[32,256]{1,0:T(8,128)} %first_ref.1, f32[1,256]{1,0:T(1,128)} %bitcast.12, bf16[256,256]{1,0:T(8,128)(2,1)} %second_ref.1, bf16[3,768,256]{2,1,0:T(8,128)(2,1)} %bitcast.8, ...), custom_call_target="tpu_custom_call" | custom-call | tf_op jit(solution)/shard_map/exchange/pallas_call | solution.py:430
  73.0 1.9 %copy.11 = bf16[24,48,256]{2,1,0:T(8,128)(2,1)} copy(bf16[24,48,256]{2,1,0:T(8,128)(2,1)} %exchange.1) | data formatting | bytes 1179648
